TPU v7x, 32 devices: a whole 2x2x4 slice. The times are simulated.
32 devices in a mesh: gx: 4 (over x, core), gy: 8 (over z, y).
Axes of the slice: x: 2, y: 2, z: 4, core: 2. Of those that a mesh axis runs over, the one named last changes fastest.
Arguments:
- thermal_departure: float32 [40, 256, 2048], P(None, 'gx', 'gy'), may hold values from -6 to 6
- current_speeds: float32 [2, 40, 256, 2048], P(None, None, 'gx', 'gy'), may hold values from -3 to 3
- mixing_coefficient: float32 [40, 256, 2048], P(None, 'gx', 'gy'), may hold values from 0.1 to 10
- seawater_indicator: int32 [256, 2048], P('gx', 'gy'), may hold values 0 or 1
- submerged_layer_tally: int32 [256, 2048], P('gx', 'gy'), may hold values from 1 to 40
- rainfall_runoff_input: float32 [256, 2048], P('gx', 'gy'), may hold values from -6 to 6
Outputs:
- temperature_next: float32 [40, 256, 2048], P(None, 'gx', 'gy')
- velocity_next: float32 [2, 40, 256, 2048], P(None, None, 'gx', 'gy')
- surface_pressure: float32 [256, 2048], P('gx', 'gy')
All inputs are finite; a program needn't handle non-finite values. No bound on the sum of `seawater_indicator` on one device may be relied on, other than what follows from the above.
Results may differ from a plain program's by a relative error of at most 0.0003.
Values sent between devices are 32-bit elements; how exact they have to be, the bound alone decides.
A program may use at most 128 MiB of HBM per device.

v0:
```python
import jax
import jax.numpy as jnp
from jax import lax
from jax.sharding import PartitionSpec as P

ITERS = 6


damping = 0.05
lower_bound = 0.02
upper_bound = 2.0
cheb_alpha = 2.0 / (upper_bound - lower_bound)
cheb_gamma = (upper_bound + lower_bound) / 2.0
advect_scale = 0.4
force_scale = 4.0
source_scale = 0.5
divergence_scale = 4.0


def padded_2(cells, sides, width):
    for axis, dim in sides:
        count = lax.axis_size(axis)
        head = lax.slice_in_dim(cells, 0, width, axis=dim)
        tail = lax.slice_in_dim(cells, cells.shape[dim] - width, cells.shape[dim], axis=dim)
        cells = jnp.concatenate(
            [
                lax.ppermute(tail, axis, [(i, (i + 1) % count) for i in range(count)]),
                cells,
                lax.ppermute(head, axis, [((i + 1) % count, i) for i in range(count)]),
            ],
            axis=dim,
        )
    return cells


def neighbor_total(padded):
    edges = (
        padded[..., 2:, 1:-1]
        + padded[..., :-2, 1:-1]
        + padded[..., 1:-1, 2:]
        + padded[..., 1:-1, :-2]
    )
    corners = (
        padded[..., 2:, 2:] + padded[..., 2:, :-2] + padded[..., :-2, 2:] + padded[..., :-2, :-2]
    )
    return edges + 0.5 * corners


def vertical_mix(source, coupling):
    count = source.shape[0]
    zeros = jnp.zeros_like(source[0])
    above = [zeros] + [coupling[level] for level in range(1, count)]
    below = above[1:] + [zeros]
    factors = []
    values = []
    for level in range(count):
        denominator = 1.0 + above[level] + below[level]
        numerator = source[level]
        if level > 0:
            denominator = denominator - above[level] * factors[-1]
            numerator = numerator + above[level] * values[-1]
        values.append(numerator / denominator)
        factors.append(below[level] / denominator)
    result = [values[-1]]
    for level in range(count - 2, -1, -1):
        result.append(values[level] + factors[level] * result[-1])
    return jnp.stack(result[::-1])


def tracer_update(extended):
    temp_ext = extended[0]
    east_vel = extended[1]
    north_vel = extended[2]
    wet_ext = (extended[3] > 0).astype(jnp.float32)
    east_open = wet_ext[:, :-1, 1:-1] * wet_ext[:, 1:, 1:-1] * east_vel[:, :-1, 1:-1]
    north_open = wet_ext[:, 1:-1, :-1] * wet_ext[:, 1:-1, 1:] * north_vel[:, 1:-1, :-1]
    flux_east = (
        jnp.maximum(east_open, 0.0) * temp_ext[:, :-1, 1:-1]
        + jnp.minimum(east_open, 0.0) * temp_ext[:, 1:, 1:-1]
    )
    flux_north = (
        jnp.maximum(north_open, 0.0) * temp_ext[:, 1:-1, :-1]
        + jnp.minimum(north_open, 0.0) * temp_ext[:, 1:-1, 1:]
    )
    convergence = (
        flux_east[:, 1:] - flux_east[:, :-1] + flux_north[:, :, 1:] - flux_north[:, :, :-1]
    )
    provisional = temp_ext[:, 1:-1, 1:-1] - advect_scale * wet_ext[:, 1:-1, 1:-1] * convergence
    temp_next = vertical_mix(provisional, extended[3][:, 1:-1, 1:-1])
    buoyancy = -temp_next
    pressure = (jnp.cumsum(buoyancy, axis=0) - 0.5 * buoyancy) / temp_next.shape[0]
    return (temp_next, pressure)


def momentum_update(extended, press_ext, ocean, rainfall_runoff_input):
    east_vel = extended[1]
    north_vel = extended[2]
    wet_ext = (extended[3] > 0).astype(jnp.float32)
    east_full = (
        wet_ext[:, :-1, 1:-1]
        * wet_ext[:, 1:, 1:-1]
        * (
            east_vel[:, :-1, 1:-1]
            + force_scale * (press_ext[:, :-1, 1:-1] - press_ext[:, 1:, 1:-1])
        )
    )
    north_full = (
        wet_ext[:, 1:-1, :-1]
        * wet_ext[:, 1:-1, 1:]
        * (
            north_vel[:, 1:-1, :-1]
            + force_scale * (press_ext[:, 1:-1, :-1] - press_ext[:, 1:-1, 1:])
        )
    )
    velocity_next = jnp.stack([east_full[:, 1:], north_full[:, :, 1:]])
    east_total = jnp.sum(east_full, axis=0) / east_full.shape[0]
    north_total = jnp.sum(north_full, axis=0) / north_full.shape[0]
    divergence = east_total[1:] - east_total[:-1] + north_total[:, 1:] - north_total[:, :-1]
    forcing = ocean * (source_scale * rainfall_runoff_input - divergence_scale * divergence)
    return (velocity_next, forcing)


def chebyshev(forcing, depth_root, total_fn):
    diag = damping + depth_root * total_fn(depth_root)
    inverse = 1.0 / diag
    update = inverse * forcing / cheb_gamma
    iterate = update
    omega = 2.0 / cheb_gamma
    for step in range(1, ITERS):
        residual = forcing - (diag * iterate - depth_root * total_fn(depth_root * iterate))
        omega = 1.0 / (cheb_gamma - omega / (4.0 * cheb_alpha * cheb_alpha))
        update = omega * inverse * residual + (cheb_gamma * omega - 1.0) * update
        iterate = iterate + update
    return iterate


def tile_total(field):
    return neighbor_total(padded_2(field, (("gx", 0), ("gy", 1)), 1))


def local(
    thermal_departure,
    current_speeds,
    mixing_coefficient,
    seawater_indicator,
    submerged_layer_tally,
    rainfall_runoff_input,
):
    layer_tally_grid, parallel_extent, meridian_extent = thermal_departure.shape
    total_y = meridian_extent * lax.axis_size("gy")
    latitude = lax.axis_index("gy") * meridian_extent + jnp.arange(meridian_extent)
    inner = (latitude > 0) & (latitude < total_y - 1)
    ocean_int = jnp.where(inner[None, :], seawater_indicator, 0)
    ocean = ocean_int.astype(jnp.float32)
    levels = jnp.arange(layer_tally_grid)[:, None, None]
    submerged_indicator = ((levels < submerged_layer_tally[None]) & (ocean_int[None] == 1)).astype(
        jnp.float32
    )
    joined_quantities = jnp.stack(
        [
            thermal_departure,
            current_speeds[0],
            current_speeds[1],
            mixing_coefficient * submerged_indicator,
        ]
    )
    extended = padded_2(joined_quantities, (("gx", 2), ("gy", 3)), 1)
    temp_next, pressure = tracer_update(extended)
    press_ext = padded_2(pressure, (("gx", 1), ("gy", 2)), 1)
    velocity_next, forcing = momentum_update(extended, press_ext, ocean, rainfall_runoff_input)
    depth_root = jnp.sqrt(
        (submerged_layer_tally * ocean_int).astype(jnp.float32) / layer_tally_grid
    )
    surface = chebyshev(forcing, depth_root, tile_total)
    return (temp_next, velocity_next, surface)


def solution(mesh):
    placed = (
        P(None, "gx", "gy"),
        P(None, None, "gx", "gy"),
        P(None, "gx", "gy"),
        P("gx", "gy"),
        P("gx", "gy"),
        P("gx", "gy"),
    )
    return jax.shard_map(
        local,
        mesh=mesh,
        in_specs=placed,
        out_specs=(P(None, "gx", "gy"), P(None, None, "gx", "gy"), P("gx", "gy")),
        check_vma=False,
    )
```

profile of v0, /device:TPU:0, one launch (start us, length us, event | category | flops | bytes accessed | tf_op | source)
XLA Modules:
  0.0 206.4 jit_solution(12069824052022272267)
XLA Ops:
  1.5 2.3 %select_bitcast_fusion = f32[1,40,64,256]{3,2,1,0:T(8,128)S(1)} fusion(f32[40,64,256]{2,1,0:T(8,128)} %param.8, s32[64,256]{1,0:T(8,128)} %param.10, pred[64,256]{1,0:T(8,128)(4,1)S(1)} %select_compare_fusion), kind=kLoop, calls=%fused_computation.40 | loop fusion | flops 1966080 | bytes 5324800 | tf_op jit(solution)/shard_map/stack | solution.py:159
  6.8 2.0 collective-permute-start.1
  9.6 3.8 %collective-permute-done.8 = f32[1,256]{1,0:T(1,128)S(1)} collective-permute-done((f32[1,256]{1,0:T(1,128)S(1)}, f32[1,256]{1,0:T(1,128)S(1)}, u32[]{:S(2)}, u32[]{:S(2)}) %collective-permute-start.8) | collective-permute-done | bytes 1056 | tf_op jit(solution)/shard_map/ppermute | solution.py:29
  13.9 5.6 %pad_maximum_fusion.1 = f32[4,40,66,256]{3,2,1,0:T(8,128)} fusion(f32[4,40,1,256]{3,2,1,0:T(1,128)S(1)} %collective-permute-done.1, f32[1,40,64,256]{3,2,1,0:T(8,128)S(1)} %select_bitcast_fusion, f32[2,40,64,256]{3,2,1,0:T(8,128)S(1)} %copy-done.1, f32[1,40,64,256]{3,2,1,0:T(8,128)S(1)} %bitcast.19, f32[4,40,1,256]{3,2,1,0:T(1,128)S(1)} %collective-permute-done), kind=kLoop, calls=%fused_computation.1 | loop fusion | flops 10813440 | bytes 21626880 | tf_op jit(solution)/shard_map/concatenate | solution.py:25
  19.5 10.2 %fusion.156 = (f32[4,40,66,1]{3,2,1,0:T(8,128)}, f32[4,40,66,1]{3,2,1,0:T(8,128)}) fusion(f32[4,40,66,256]{3,2,1,0:T(8,128)} %pad_maximum_fusion.1), kind=kLoop, calls=%fused_computation.410 | loop fusion | bytes 168960 | tf_op jit(solution)/shard_map/slice | solution.py:24
  29.8 3.8 %copy.9 = f32[4,40,66,1]{2,1,3,0:T(8,128)S(1)} copy(f32[4,40,66,1]{3,2,1,0:T(8,128)} %get-tuple-element.118) | data formatting | bytes 84480 | tf_op jit(solution)/shard_map/slice | solution.py:24
  35.1 3.8 %copy.10 = f32[4,40,66,1]{2,1,3,0:T(8,128)S(1)} copy(f32[4,40,66,1]{3,2,1,0:T(8,128)} %get-tuple-element.119) | data formatting | bytes 84480 | tf_op jit(solution)/shard_map/slice | solution.py:23
  38.9 3.3 %collective-permute-start.3 = (f32[4,40,66,1]{2,1,3,0:T(8,128)S(1)}, f32[4,40,66,1]{2,1,3,0:T(8,128)S(1)}, u32[]{:S(2)}, u32[]{:S(2)}) collective-permute-start(f32[4,40,66,1]{2,1,3,0:T(8,128)S(1)} %copy.10), channel_id=1, source_target_pairs={{1,0},{2,1},{3,2},{4,3},{5,4},{6,5},{7,6},{0,7},{9,8},{10,9},{11,1... | collective-permute-start | bytes 126728 | tf_op jit(solution)/shard_map/ppermute | solution.py:29
  44.8 3.7 %copy.11 = f32[4,40,66,1]{3,2,1,0:T(8,128)} copy(f32[4,40,66,1]{2,1,3,0:T(8,128)S(1)} %collective-permute-done.2) | data formatting | bytes 84480 | tf_op jit(solution)/shard_map/ppermute | solution.py:27
  48.6 3.6 %copy.12 = f32[4,40,66,1]{3,2,1,0:T(8,128)} copy(f32[4,40,66,1]{2,1,3,0:T(8,128)S(1)} %collective-permute-done.3) | data formatting | bytes 84480 | tf_op jit(solution)/shard_map/ppermute | solution.py:29
  52.2 18.7 %pad_maximum_fusion = f32[4,40,66,258]{3,2,1,0:T(8,128)} fusion(f32[4,40,66,1]{3,2,1,0:T(8,128)} %copy.12, f32[4,40,1,256]{3,2,1,0:T(1,128)S(1)} %collective-permute-done.1, f32[1,40,64,256]{3,2,1,0:T(8,128)S(1)} %select_bitcast_fusion, f32[2,40,64,256]{3,2,1,0:T(8,128)} %param.7, f32[1,40,64,256]{3,2,1,0:T(8,128)} %bitcast.18, ...), kind=kLoop, calls=%fused_computation | loop fusion | flops 16346880 | bytes 21795840 | tf_op jit(solution)/shard_map/concatenate | solution.py:25
  70.9 8.8 %slice_bitcast_fusion.1 = (f32[40,66,258]{2,1,0:T(8,128)S(1)}, f32[40,66,258]{2,1,0:T(8,128)S(1)}, f32[40,66,258]{2,1,0:T(8,128)}, f32[40,66,258]{2,1,0:T(8,128)S(1)}) fusion(f32[4,40,66,258]{3,2,1,0:T(8,128)} %pad_maximum_fusion), kind=kLoop, calls=%fused_computation.4 | loop fusion | bytes 21795840 | tf_op jit(solution)/shard_map/squeeze | solution.py:72
  79.8 5.7 %compare_convert_fusion = f32[40,66,258]{2,1,0:T(8,128)S(1)} fusion(f32[4,40,66,258]{3,2,1,0:T(8,128)} %pad_maximum_fusion), kind=kLoop, calls=%fused_computation.7 | loop fusion | flops 1362240 | bytes 5448960 | tf_op jit(solution)/shard_map/convert_element_type | solution.py:74
  85.5 5.5 %fusion.5 = f32[40,65,256]{2,1,0:T(8,128)} fusion(f32[40,66,258]{2,1,0:T(8,128)S(1)} %get-tuple-element.117, f32[40,66,258]{2,1,0:T(8,128)S(1)} %get-tuple-element.114, f32[40,66,258]{2,1,0:T(8,128)S(1)} %compare_convert_fusion), kind=kLoop, calls=%fused_computation.23 | loop fusion | flops 4659200 | bytes 15974400 | tf_op jit(solution)/shard_map/add | solution.py:78
  91.0 5.1 %fusion.4 = f32[40,64,257]{2,1,0:T(8,128)} fusion(f32[40,66,258]{2,1,0:T(8,128)S(1)} %get-tuple-element.117, f32[40,66,258]{2,1,0:T(8,128)S(1)} %get-tuple-element.115, f32[40,66,258]{2,1,0:T(8,128)S(1)} %compare_convert_fusion), kind=kLoop, calls=%fused_computation.19 | loop fusion | flops 4605440 | bytes 15790080 | tf_op jit(solution)/shard_map/add | solution.py:82
  96.1 8.7 %fusion.10 = f32[40,64,256]{2,1,0:T(8,128)} fusion(f32[40,64,257]{2,1,0:T(8,128)} %fusion.4, f32[40,65,256]{2,1,0:T(8,128)} %fusion.5, f32[40,66,258]{2,1,0:T(8,128)S(1)} %compare_convert_fusion, f32[40,66,258]{2,1,0:T(8,128)S(1)} %get-tuple-element.117), kind=kLoop, calls=%fused_computation.35 | loop fusion | flops 3932160 | bytes 18350080 | tf_op jit(solution)/shard_map/sub | solution.py:88
  104.8 4.2 %fusion.68 = (f32[1,64,256]{2,1,0:T(8,128)S(1)}, f32[1,64,256]{2,1,0:T(8,128)S(1)}, f32[1,64,256]{2,1,0:T(8,128)S(1)}, f32[1,64,256]{2,1,0:T(8,128)S(1)}, f32[1,...) fusion(f32[40,64,256]{2,1,0:T(8,128)} %fusion.10, ...), kind=kLoop, calls=%fused_computation.209 | loop fusion | flops 4866048 | bytes 9699328 | tf_op jit(solution)/shard_map/div | solution.py:62
  109.0 2.6 %constant_dynamic-update-slice_fusion.39 = (f32[40,64,256]{2,1,0:T(8,128)S(1)}, f32[1,64,256]{2,1,0:T(8,128)S(1)}, f32[1,64,256]{2,1,0:T(8,128)S(1)}, f32[1,64,2...) fusion(f32[40,66,258]{2,1,0:T(8,128)} %get-tuple-element.116, ...), kind=kLoop, calls=%fused_computation.102 | loop fusion | flops 1966079 | bytes 7798784
  120.0 2.1 fusion.157
  125.9 4.7 %collective-permute-start.7 = (f32[40,66,1]{1,0,2:T(8,128)S(1)}, f32[40,66,1]{1,0,2:T(8,128)S(1)}, u32[]{:S(2)}, u32[]{:S(2)}) collective-permute-start(f32[40,66,1]{1,0,2:T(8,128)S(1)} %copy.15), channel_id=1, source_target_pairs={{1,0},{2,1},{3,2},{4,3},{5,4},{6,5},{7,6},{0,7},{9,8},{10,9},{11,1... | collective-permute-start | bytes 31688 | tf_op jit(solution)/shard_map/ppermute | solution.py:29
  130.6 8.5 %fusion.117 = (f32[65,256]{1,0:T(8,128)S(1)}, f32[40,65,256]{2,1,0:T(8,128)}) fusion(f32[40,1,256]{2,1,0:T(1,128)S(1)} %collective-permute-done.5, f32[40,64,256]{2,1,0:T(8,128)S(1)} %subtract_multiply_fusion, f32[40,1,256]{2,1,0:T(1,128)S(1)} %collective-permute-done.4, f32[40,66,258]{2,1,0:T(8,128)} %copy-done.3, f32[40,66,258]{2,1,0:T(8,128)} %copy-done), kind=kLoop, calls=%fused_computation.408 | loop fusion | flops 5308160 | bytes 13419520 | tf_op jit(solution)/shard_map/reduce_sum | solution.py:116
  142.6 9.0 %fusion.119 = (f32[64,257]{1,0:T(8,128)S(1)}, f32[40,64,257]{2,1,0:T(8,128)S(1)}) fusion(f32[40,66,1]{2,1,0:T(8,128)} %copy.16, f32[40,1,256]{2,1,0:T(1,128)S(1)} %collective-permute-done.5, f32[40,64,256]{2,1,0:T(8,128)S(1)} %subtract_multiply_fusion, f32[40,1,256]{2,1,0:T(1,128)S(1)} %collective-permute-done.4, f32[40,66,1]{2,1,0:T(8,128)} %copy.14, ...), kind=kLoop, calls=%fused_computation.409 | loop fusion | flops 7878592 | bytes 13316992 | tf_op jit(solution)/shard_map/reduce_sum | solution.py:117
  160.6 3.9 %collective-permute-done.15 = f32[66,1]{1,0:T(8,128)S(1)} collective-permute-done((f32[66,1]{1,0:T(8,128)S(1)}, f32[66,1]{1,0:T(8,128)S(1)}, u32[]{:S(2)}, u32[]{:S(2)}) %collective-permute-start.15) | collective-permute-done | bytes 296 | tf_op jit(solution)/shard_map/ppermute | solution.py:27
  168.2 2.0 collective-permute-start.19
  172.2 2.8 %collective-permute-done.19 = f32[66,1]{1,0:T(8,128)S(1)} collective-permute-done((f32[66,1]{1,0:T(8,128)S(1)}, f32[66,1]{1,0:T(8,128)S(1)}, u32[]{:S(2)}, u32[]{:S(2)}) %collective-permute-start.19) | collective-permute-done | bytes 296 | tf_op jit(solution)/shard_map/ppermute | solution.py:27
  178.4 2.0 collective-permute-start.23
  182.4 2.8 %collective-permute-done.23 = f32[66,1]{1,0:T(8,128)S(1)} collective-permute-done((f32[66,1]{1,0:T(8,128)S(1)}, f32[66,1]{1,0:T(8,128)S(1)}, u32[]{:S(2)}, u32[]{:S(2)}) %collective-permute-start.23) | collective-permute-done | bytes 296 | tf_op jit(solution)/shard_map/ppermute | solution.py:27
  188.6 2.0 collective-permute-start.27
  192.6 2.8 %collective-permute-done.27 = f32[66,1]{1,0:T(8,128)S(1)} collective-permute-done((f32[66,1]{1,0:T(8,128)S(1)}, f32[66,1]{1,0:T(8,128)S(1)}, u32[]{:S(2)}, u32[]{:S(2)}) %collective-permute-start.27) | collective-permute-done | bytes 296 | tf_op jit(solution)/shard_map/ppermute | solution.py:27
  198.8 2.0 collective-permute-start.31
  200.8 2.7 %pad_maximum_fusion.2 = f32[2,40,64,256]{3,2,1,0:T(8,128)} fusion(f32[1,40,64,256]{3,2,1,0:T(8,128)S(1)} %get-tuple-element.163, f32[1,40,64,256]{3,2,1,0:T(8,128)S(1)} %get-tuple-element.164), kind=kLoop, calls=%fused_computation.2 | loop fusion | flops 1310720 | bytes 10485760 | tf_op jit(solution)/shard_map/stack | solution.py:115
  203.5 2.0 collective-permute-done.31
  (166 shorter events, 54.2 us)
Async XLA Ops:
  6.3 7.1 %collective-permute-start = (f32[4,40,1,256]{3,2,1,0:T(1,128)S(1)}, f32[4,40,1,256]{3,2,1,0:T(1,128)S(1)}, u32[]{:S(2)}, u32[]{:S(2)}) collective-permute-start(f32[4,40,1,256]{3,2,1,0:T(1,128)S(1)} %get-tuple-element.120), channel_id=1, source_target_pairs={{0,8},{8,16},{16,24},{24,0},{1,9},{9,17},{17,25},{25,1},{2,10},{10... | collective-permute-start | bytes 491528 | tf_op jit(solution)/shard_map/ppermute | solution.py:27
  6.8 7.1 %collective-permute-start.1 = (f32[4,40,1,256]{3,2,1,0:T(1,128)S(1)}, f32[4,40,1,256]{3,2,1,0:T(1,128)S(1)}, u32[]{:S(2)}, u32[]{:S(2)}) collective-permute-start(f32[4,40,1,256]{3,2,1,0:T(1,128)S(1)} %get-tuple-element.121), channel_id=1, source_target_pairs={{8,0},{16,8},{24,16},{0,24},{9,1},{17,9},{25,17},{1,25},{10,2},{18... | collective-permute-start | bytes 491528 | tf_op jit(solution)/shard_map/ppermute | solution.py:29
  8.8 4.5 %collective-permute-start.8 = (f32[1,256]{1,0:T(1,128)S(1)}, f32[1,256]{1,0:T(1,128)S(1)}, u32[]{:S(2)}, u32[]{:S(2)}) collective-permute-start(f32[1,256]{1,0:T(1,128)S(1)} %get-tuple-element.161), channel_id=1, source_target_pairs={{8,0},{16,8},{24,16},{0,24},{9,1},{17,9},{25,17},{1,25},{10,2},{18... | collective-permute-start | bytes 3080 | tf_op jit(solution)/shard_map/ppermute | solution.py:29
  9.6 3.8 %collective-permute-start.9 = (f32[1,256]{1,0:T(1,128)S(1)}, f32[1,256]{1,0:T(1,128)S(1)}, u32[]{:S(2)}, u32[]{:S(2)}) collective-permute-start(f32[1,256]{1,0:T(1,128)S(1)} %get-tuple-element.160), channel_id=1, source_target_pairs={{0,8},{8,16},{16,24},{24,0},{1,9},{9,17},{17,25},{25,1},{2,10},{10... | collective-permute-start | bytes 3080 | tf_op jit(solution)/shard_map/ppermute | solution.py:27
  33.5 11.3 %collective-permute-start.2 = (f32[4,40,66,1]{2,1,3,0:T(8,128)S(1)}, f32[4,40,66,1]{2,1,3,0:T(8,128)S(1)}, u32[]{:S(2)}, u32[]{:S(2)}) collective-permute-start(f32[4,40,66,1]{2,1,3,0:T(8,128)S(1)} %copy.9), channel_id=1, source_target_pairs={{0,1},{1,2},{2,3},{3,4},{4,5},{5,6},{6,7},{7,0},{8,9},{9,10},{10,1... | collective-permute-start | bytes 126728 | tf_op jit(solution)/shard_map/ppermute | solution.py:27
  38.9 9.6 %collective-permute-start.3 = (f32[4,40,66,1]{2,1,3,0:T(8,128)S(1)}, f32[4,40,66,1]{2,1,3,0:T(8,128)S(1)}, u32[]{:S(2)}, u32[]{:S(2)}) collective-permute-start(f32[4,40,66,1]{2,1,3,0:T(8,128)S(1)} %copy.10), channel_id=1, source_target_pairs={{1,0},{2,1},{3,2},{4,3},{5,4},{6,5},{7,6},{0,7},{9,8},{10,9},{11,1... | collective-permute-start | bytes 126728 | tf_op jit(solution)/shard_map/ppermute | solution.py:29
  42.8 75.0 %collective-permute-start.10 = (f32[66,1]{1,0:T(8,128)}, f32[66,1]{1,0:T(8,128)S(1)}, u32[]{:S(2)}, u32[]{:S(2)}) collective-permute-start(f32[66,1]{1,0:T(8,128)} %get-tuple-element.136), channel_id=1, source_target_pairs={{1,0},{2,1},{3,2},{4,3},{5,4},{6,5},{7,6},{0,7},{9,8},{10,9},{11,1... | collective-permute-start | bytes 800 | tf_op jit(solution)/shard_map/ppermute | solution.py:29
  44.6 73.1 %collective-permute-start.11 = (f32[66,1]{1,0:T(8,128)S(1)}, f32[66,1]{1,0:T(8,128)}, u32[]{:S(2)}, u32[]{:S(2)}) collective-permute-start(f32[66,1]{1,0:T(8,128)S(1)} %get-tuple-element.137), channel_id=1, source_target_pairs={{0,1},{1,2},{2,3},{3,4},{4,5},{5,6},{6,7},{7,0},{8,9},{9,10},{10,1... | collective-permute-start | bytes 800 | tf_op jit(solution)/shard_map/ppermute | solution.py:27
  115.9 3.5 %collective-permute-start.4 = (f32[40,1,256]{2,1,0:T(1,128)S(1)}, f32[40,1,256]{2,1,0:T(1,128)S(1)}, u32[]{:S(2)}, u32[]{:S(2)}) collective-permute-start(f32[40,1,256]{2,1,0:T(1,128)S(1)} %get-tuple-element.124), channel_id=1, source_target_pairs={{0,8},{8,16},{16,24},{24,0},{1,9},{9,17},{17,25},{25,1},{2,10},{10... | collective-permute-start | bytes 122888 | tf_op jit(solution)/shard_map/ppermute | solution.py:27
  116.0 3.6 %collective-permute-start.5 = (f32[40,1,256]{2,1,0:T(1,128)S(1)}, f32[40,1,256]{2,1,0:T(1,128)S(1)}, u32[]{:S(2)}, u32[]{:S(2)}) collective-permute-start(f32[40,1,256]{2,1,0:T(1,128)S(1)} %get-tuple-element.125), channel_id=1, source_target_pairs={{8,0},{16,8},{24,16},{0,24},{9,1},{17,9},{25,17},{1,25},{10,2},{18... | collective-permute-start | bytes 122888 | tf_op jit(solution)/shard_map/ppermute | solution.py:29
  123.9 15.2 %collective-permute-start.6 = (f32[40,66,1]{1,0,2:T(8,128)S(1)}, f32[40,66,1]{1,0,2:T(8,128)S(1)}, u32[]{:S(2)}, u32[]{:S(2)}) collective-permute-start(f32[40,66,1]{1,0,2:T(8,128)S(1)} %copy.13), channel_id=1, source_target_pairs={{0,1},{1,2},{2,3},{3,4},{4,5},{5,6},{6,7},{7,0},{8,9},{9,10},{10,1... | collective-permute-start | bytes 31688 | tf_op jit(solution)/shard_map/ppermute | solution.py:27
  125.9 15.0 %collective-permute-start.7 = (f32[40,66,1]{1,0,2:T(8,128)S(1)}, f32[40,66,1]{1,0,2:T(8,128)S(1)}, u32[]{:S(2)}, u32[]{:S(2)}) collective-permute-start(f32[40,66,1]{1,0,2:T(8,128)S(1)} %copy.15), channel_id=1, source_target_pairs={{1,0},{2,1},{3,2},{4,3},{5,4},{6,5},{7,6},{0,7},{9,8},{10,9},{11,1... | collective-permute-start | bytes 31688 | tf_op jit(solution)/shard_map/ppermute | solution.py:29
  151.8 3.0 %collective-permute-start.12 = (f32[1,256]{1,0:T(1,128)S(1)}, f32[1,256]{1,0:T(1,128)S(1)}, u32[]{:S(2)}, u32[]{:S(2)}) collective-permute-start(f32[1,256]{1,0:T(1,128)S(1)} %get-tuple-element.159), channel_id=1, source_target_pairs={{8,0},{16,8},{24,16},{0,24},{9,1},{17,9},{25,17},{1,25},{10,2},{18... | collective-permute-start | bytes 3080 | tf_op jit(solution)/shard_map/ppermute | solution.py:29
  153.5 3.0 %collective-permute-start.13 = (f32[1,256]{1,0:T(1,128)S(1)}, f32[1,256]{1,0:T(1,128)S(1)}, u32[]{:S(2)}, u32[]{:S(2)}) collective-permute-start(f32[1,256]{1,0:T(1,128)S(1)} %get-tuple-element.158), channel_id=1, source_target_pairs={{0,8},{8,16},{16,24},{24,0},{1,9},{9,17},{17,25},{25,1},{2,10},{10... | collective-permute-start | bytes 3080 | tf_op jit(solution)/shard_map/ppermute | solution.py:27
  156.6 4.0 %collective-permute-start.14 = (f32[66,1]{1,0:T(8,128)S(1)}, f32[66,1]{1,0:T(8,128)S(1)}, u32[]{:S(2)}, u32[]{:S(2)}) collective-permute-start(f32[66,1]{1,0:T(8,128)S(1)} %get-tuple-element.134), channel_id=1, source_target_pairs={{1,0},{2,1},{3,2},{4,3},{5,4},{6,5},{7,6},{0,7},{9,8},{10,9},{11,1... | collective-permute-start | bytes 800 | tf_op jit(solution)/shard_map/ppermute | solution.py:29
  157.8 6.7 %collective-permute-start.15 = (f32[66,1]{1,0:T(8,128)S(1)}, f32[66,1]{1,0:T(8,128)S(1)}, u32[]{:S(2)}, u32[]{:S(2)}) collective-permute-start(f32[66,1]{1,0:T(8,128)S(1)} %get-tuple-element.135), channel_id=1, source_target_pairs={{0,1},{1,2},{2,3},{3,4},{4,5},{5,6},{6,7},{7,0},{8,9},{9,10},{10,1... | collective-permute-start | bytes 800 | tf_op jit(solution)/shard_map/ppermute | solution.py:27
  164.8 1.4 collective-permute-start.16
  164.8 3.0 %collective-permute-start.17 = (f32[1,256]{1,0:T(1,128)S(1)}, f32[1,256]{1,0:T(1,128)S(1)}, u32[]{:S(2)}, u32[]{:S(2)}) collective-permute-start(f32[1,256]{1,0:T(1,128)S(1)} %get-tuple-element.156), channel_id=1, source_target_pairs={{0,8},{8,16},{16,24},{24,0},{1,9},{9,17},{17,25},{25,1},{2,10},{10... | collective-permute-start | bytes 3080 | tf_op jit(solution)/shard_map/ppermute | solution.py:27
  168.0 4.2 %collective-permute-start.18 = (f32[66,1]{1,0:T(8,128)S(1)}, f32[66,1]{1,0:T(8,128)S(1)}, u32[]{:S(2)}, u32[]{:S(2)}) collective-permute-start(f32[66,1]{1,0:T(8,128)S(1)} %get-tuple-element.132), channel_id=1, source_target_pairs={{1,0},{2,1},{3,2},{4,3},{5,4},{6,5},{7,6},{0,7},{9,8},{10,9},{11,1... | collective-permute-start | bytes 800 | tf_op jit(solution)/shard_map/ppermute | solution.py:29
  168.2 6.7 %collective-permute-start.19 = (f32[66,1]{1,0:T(8,128)S(1)}, f32[66,1]{1,0:T(8,128)S(1)}, u32[]{:S(2)}, u32[]{:S(2)}) collective-permute-start(f32[66,1]{1,0:T(8,128)S(1)} %get-tuple-element.133), channel_id=1, source_target_pairs={{0,1},{1,2},{2,3},{3,4},{4,5},{5,6},{6,7},{7,0},{8,9},{9,10},{10,1... | collective-permute-start | bytes 800 | tf_op jit(solution)/shard_map/ppermute | solution.py:27
  175.2 1.4 collective-permute-start.20
  175.3 3.0 %collective-permute-start.21 = (f32[1,256]{1,0:T(1,128)S(1)}, f32[1,256]{1,0:T(1,128)S(1)}, u32[]{:S(2)}, u32[]{:S(2)}) collective-permute-start(f32[1,256]{1,0:T(1,128)S(1)} %get-tuple-element.154), channel_id=1, source_target_pairs={{0,8},{8,16},{16,24},{24,0},{1,9},{9,17},{17,25},{25,1},{2,10},{10... | collective-permute-start | bytes 3080 | tf_op jit(solution)/shard_map/ppermute | solution.py:27
  178.4 4.0 %collective-permute-start.22 = (f32[66,1]{1,0:T(8,128)S(1)}, f32[66,1]{1,0:T(8,128)S(1)}, u32[]{:S(2)}, u32[]{:S(2)}) collective-permute-start(f32[66,1]{1,0:T(8,128)S(1)} %get-tuple-element.130), channel_id=1, source_target_pairs={{1,0},{2,1},{3,2},{4,3},{5,4},{6,5},{7,6},{0,7},{9,8},{10,9},{11,1... | collective-permute-start | bytes 800 | tf_op jit(solution)/shard_map/ppermute | solution.py:29
  178.4 6.7 %collective-permute-start.23 = (f32[66,1]{1,0:T(8,128)S(1)}, f32[66,1]{1,0:T(8,128)S(1)}, u32[]{:S(2)}, u32[]{:S(2)}) collective-permute-start(f32[66,1]{1,0:T(8,128)S(1)} %get-tuple-element.131), channel_id=1, source_target_pairs={{0,1},{1,2},{2,3},{3,4},{4,5},{5,6},{6,7},{7,0},{8,9},{9,10},{10,1... | collective-permute-start | bytes 800 | tf_op jit(solution)/shard_map/ppermute | solution.py:27
  185.4 1.4 collective-permute-start.24
  185.5 3.0 %collective-permute-start.25 = (f32[1,256]{1,0:T(1,128)S(1)}, f32[1,256]{1,0:T(1,128)S(1)}, u32[]{:S(2)}, u32[]{:S(2)}) collective-permute-start(f32[1,256]{1,0:T(1,128)S(1)} %get-tuple-element.152), channel_id=1, source_target_pairs={{0,8},{8,16},{16,24},{24,0},{1,9},{9,17},{17,25},{25,1},{2,10},{10... | collective-permute-start | bytes 3080 | tf_op jit(solution)/shard_map/ppermute | solution.py:27
  188.6 4.0 %collective-permute-start.26 = (f32[66,1]{1,0:T(8,128)S(1)}, f32[66,1]{1,0:T(8,128)S(1)}, u32[]{:S(2)}, u32[]{:S(2)}) collective-permute-start(f32[66,1]{1,0:T(8,128)S(1)} %get-tuple-element.128), channel_id=1, source_target_pairs={{1,0},{2,1},{3,2},{4,3},{5,4},{6,5},{7,6},{0,7},{9,8},{10,9},{11,1... | collective-permute-start | bytes 800 | tf_op jit(solution)/shard_map/ppermute | solution.py:29
  188.6 6.7 %collective-permute-start.27 = (f32[66,1]{1,0:T(8,128)S(1)}, f32[66,1]{1,0:T(8,128)S(1)}, u32[]{:S(2)}, u32[]{:S(2)}) collective-permute-start(f32[66,1]{1,0:T(8,128)S(1)} %get-tuple-element.129), channel_id=1, source_target_pairs={{0,1},{1,2},{2,3},{3,4},{4,5},{5,6},{6,7},{7,0},{8,9},{9,10},{10,1... | collective-permute-start | bytes 800 | tf_op jit(solution)/shard_map/ppermute | solution.py:27
  195.6 1.6 collective-permute-start.28
  195.6 3.0 %collective-permute-start.29 = (f32[1,256]{1,0:T(1,128)S(1)}, f32[1,256]{1,0:T(1,128)S(1)}, u32[]{:S(2)}, u32[]{:S(2)}) collective-permute-start(f32[1,256]{1,0:T(1,128)S(1)} %get-tuple-element.150), channel_id=1, source_target_pairs={{0,8},{8,16},{16,24},{24,0},{1,9},{9,17},{17,25},{25,1},{2,10},{10... | collective-permute-start | bytes 3080 | tf_op jit(solution)/shard_map/ppermute | solution.py:27
  198.8 4.7 %collective-permute-start.30 = (f32[66,1]{1,0:T(8,128)S(1)}, f32[66,1]{1,0:T(8,128)S(1)}, u32[]{:S(2)}, u32[]{:S(2)}) collective-permute-start(f32[66,1]{1,0:T(8,128)S(1)} %get-tuple-element.126), channel_id=1, source_target_pairs={{1,0},{2,1},{3,2},{4,3},{5,4},{6,5},{7,6},{0,7},{9,8},{10,9},{11,1... | collective-permute-start | bytes 800 | tf_op jit(solution)/shard_map/ppermute | solution.py:29
  198.8 6.7 %collective-permute-start.31 = (f32[66,1]{1,0:T(8,128)S(1)}, f32[66,1]{1,0:T(8,128)S(1)}, u32[]{:S(2)}, u32[]{:S(2)}) collective-permute-start(f32[66,1]{1,0:T(8,128)S(1)} %get-tuple-element.127), channel_id=1, source_target_pairs={{0,1},{1,2},{2,3},{3,4},{4,5},{5,6},{6,7},{7,0},{8,9},{9,10},{10,1... | collective-permute-start | bytes 800 | tf_op jit(solution)/shard_map/ppermute | solution.py:27
  (16 other events, 114.9 us)
where the time goes:
time: 207 us; the launch traced here: 206 us
  other arithmetic  87.3 us (42%)
  local copies, waits for them, and re-layouts  47.9 us (23%)
  waiting for transfers between devices  38.6 us (19%)
  starting transfers between devices  31.1 us (15%)
    concatenate x15, other arithmetic, padded_2(): jnp.concatenate([lax.ppermute(tail, axis, [(i, (i + 1) % count) for i in...  26.2 us
    ppermute x16, waiting for transfers between devices, padded_2(): lax.ppermute(tail, axis, [(i, (i + 1) % count) for i in range(count)])  23.4 us
    slice x11, local copies, waits for them, and re-layouts, padded_2(): lax.slice_in_dim(cells, cells.shape[dim] - width, cells.shape[dim], axis=...  18.1 us
    ppermute x16, starting transfers between devices, padded_2(): lax.ppermute(head, axis, [((i + 1) % count, i) for i in range(count)])  17.7 us
    ppermute x16, waiting for transfers between devices, padded_2(): lax.ppermute(head, axis, [((i + 1) % count, i) for i in range(count)])  15.2 us
    ppermute x16, starting transfers between devices, padded_2(): lax.ppermute(tail, axis, [(i, (i + 1) % count) for i in range(count)])  13.4 us
    reduce_sum x1, other arithmetic, momentum_update(): north_total = jnp.sum(north_full, axis=0) / north_full.shape[0]  9.02 us
    squeeze x1, local copies, waits for them, and re-layouts, tracer_update(): east_vel = extended[1]  8.85 us
  transfers between devices with their start and end apart: 32, of which 21 were waited for; matrix products, arithmetic and copies ran while one was open for 44% of the time, Pallas kernels for 0%

commit v1 on v0

v1 whole, which is shorter than its diff:
```python
import functools

import jax
import jax.numpy as jnp
from jax import lax
from jax.experimental import pallas as pl
from jax.experimental.pallas import tpu as pltpu
from jax.sharding import PartitionSpec as P

ITERS = 6
damping = 0.05
lower_bound = 0.02
upper_bound = 2.0
cheb_alpha = 2.0 / (upper_bound - lower_bound)
cheb_gamma = (upper_bound + lower_bound) / 2.0
advect_scale = 0.4
force_scale = 4.0
source_scale = 0.5
divergence_scale = 4.0

MESH = pl.DeviceIdType.MESH
LANES = 128
HALF = LANES // 2
BAND = 8
F32 = jnp.float32
AROUND = ((1, 0), (-1, 0), (0, 1), (0, -1), (1, 1), (1, -1), (-1, 1), (-1, -1))


def device_at(dx, dy):
    nx, ny = lax.axis_size("gx"), lax.axis_size("gy")
    return (
        lax.rem(lax.axis_index("gx") + (dx + nx), nx),
        lax.rem(lax.axis_index("gy") + (dy + ny), ny),
    )


def meet_neighbours():
    barrier = pltpu.get_barrier_semaphore()
    for dx, dy in AROUND:
        pl.semaphore_signal(barrier, inc=1, device_id=device_at(dx, dy), device_id_type=MESH)
    pl.semaphore_wait(barrier, len(AROUND))


def send(src, dst, sems, at, dx, dy):
    copy = pltpu.make_async_remote_copy(
        src_ref=src,
        dst_ref=dst,
        send_sem=sems.at[0, at],
        recv_sem=sems.at[1, at],
        device_id=device_at(dx, dy),
        device_id_type=MESH,
    )
    copy.start()
    return copy


def halo_shapes(rows, cols):
    return [
        pltpu.VMEM((2, 2, BAND, cols), F32),
        pltpu.VMEM((2, 2, rows, LANES), F32),
        pltpu.VMEM((4, 2, BAND, LANES), F32),
        pltpu.SemaphoreType.DMA((2, 8)),
    ]


def start_halo(pair, bands, sides, corners, sems):
    rows, cols = pair.shape[1:]
    low, high = pl.ds(0, BAND), pl.ds(rows - BAND, BAND)
    left, right = pl.ds(0, LANES), pl.ds(cols - LANES, LANES)
    return [
        send(pair.at[:, low, :], bands.at[0], sems, 0, -1, 0),
        send(pair.at[:, high, :], bands.at[1], sems, 1, 1, 0),
        send(pair.at[:, :, left], sides.at[0], sems, 2, 0, -1),
        send(pair.at[:, :, right], sides.at[1], sems, 3, 0, 1),
        send(pair.at[:, low, left], corners.at[0], sems, 4, -1, -1),
        send(pair.at[:, low, right], corners.at[1], sems, 5, -1, 1),
        send(pair.at[:, high, left], corners.at[2], sems, 6, 1, -1),
        send(pair.at[:, high, right], corners.at[3], sems, 7, 1, 1),
    ]


def lane_index(shape):
    return lax.broadcasted_iota(jnp.int32, shape, len(shape) - 1)


def row_index(shape):
    return lax.broadcasted_iota(jnp.int32, shape, len(shape) - 2)


def joined(which, pair, bands, sides, corners):
    def lanes(own, north, south):
        return jnp.concatenate(
            [own, jnp.where(lane_index(north.shape) < HALF, north, south)], axis=1
        )

    return jnp.concatenate(
        [
            lanes(pair[which], sides[0, which], sides[1, which]),
            lanes(bands[0, which], corners[0, which], corners[1, which]),
            lanes(bands[1, which], corners[2, which], corners[3, which]),
        ],
        axis=0,
    )


def after(field, axis):
    return pltpu.roll(field, field.shape[axis] - 1, axis)


def before(field, axis):
    return pltpu.roll(field, 1, axis)


def around_total(field):
    pair = after(field, 0) + before(field, 0)
    slanted = field + 0.5 * pair
    return pair + after(slanted, 1) + before(slanted, 1)


def inverse_of(value):
    near = pl.reciprocal(value, approx=True)
    return near * (2.0 - value * near)


def columns_kernel(
    temp_hbm,
    speed_hbm,
    mix_hbm,
    sea,
    tally,
    rain,
    temp_out,
    speed_out,
    totals_out,
    root_out,
    inverse_out,
    source_out,
    temp,
    east,
    north,
    mix,
    factor,
    value,
    depth,
    depth_e,
    depth_n,
    surf,
    row_east,
    row_west,
    from_west,
    from_east,
    col_north,
    col_south,
    from_south,
    from_north,
    flux_west,
    flux_south,
    row_press,
    press_east,
    col_press,
    press_north,
    load_sems,
    edge_sems,
    bands,
    sides,
    corners,
    halo_sems,
):
    levels, rows, cols = temp.shape
    chunk = 8
    chunks = levels // chunk
    loads = []
    for at in range(chunks):
        part = pl.ds(at * chunk, chunk)
        loads.append(
            [
                pltpu.make_async_copy(src, dst.at[part], load_sems.at[at, which])
                for which, (src, dst) in enumerate(
                    (
                        (temp_hbm.at[part], temp),
                        (speed_hbm.at[0, part], east),
                        (speed_hbm.at[1, part], north),
                        (mix_hbm.at[part], mix),
                    )
                )
            ]
        )
        for copy in loads[-1]:
            copy.start()

    tile = (rows, cols)
    latitude = lax.axis_index("gy") * cols + lane_index(tile)
    inner = (latitude > 0) & (latitude < cols * lax.axis_size("gy") - 1)
    wet_levels = jnp.where(inner & (sea[...] == 1), tally[...], 0).astype(F32)
    depth[...] = wet_levels
    surf[0] = wet_levels
    surf[1] = rain[...]

    meet_neighbours()
    surf_copies = start_halo(surf, bands, sides, corners, halo_sems)

    lane = lane_index((rows, LANES))
    zero_side = jnp.zeros((rows, LANES), F32)

    def pack(k, carry):
        to_north, to_south = carry
        one = pl.ds(k, 1)
        row_east[0, one, :] = temp[k, rows - 1 : rows, :]
        row_east[1, one, :] = east[k, rows - 1 : rows, :]
        row_west[one, :] = temp[k, 0:1, :]
        to_north = jnp.where(
            lane == k, pltpu.roll(temp[k, :, cols - LANES :], k + 1, 1), to_north
        )
        to_north = jnp.where(
            lane == k + HALF, pltpu.roll(north[k, :, cols - LANES :], k + 1 + HALF, 1), to_north
        )
        to_south = jnp.where(lane == k, pltpu.roll(temp[k, :, :LANES], k, 1), to_south)
        return to_north, to_south

    carry = (zero_side, zero_side)
    for at in range(chunks):
        for copy in loads[at][:3]:
            copy.wait()
        carry = lax.fori_loop(at * chunk, (at + 1) * chunk, pack, carry)
    col_north[...], col_south[...] = carry
    edges = [
        send(row_east, from_west, edge_sems, 0, 1, 0),
        send(row_west, from_east, edge_sems, 1, -1, 0),
        send(col_north, from_south, edge_sems, 2, 0, 1),
        send(col_south, from_north, edge_sems, 3, 0, -1),
    ]

    for copy in surf_copies:
        copy.wait()
    wide = joined(0, surf, bands, sides, corners)
    root = jnp.sqrt(wide / levels)
    root_out[...] = root
    inverse_out[...] = 1.0 / (damping + root * around_total(root))
    source_out[...] = source_scale * joined(1, surf, bands, sides, corners)
    depth_e[...] = jnp.minimum(wide, after(wide, 0))[:rows, :cols]
    depth_n[...] = jnp.minimum(wide, after(wide, 1))[:rows, :cols]
    west_depth = jnp.minimum(wide, before(wide, 0))[0:1, :cols]
    south_depth = jnp.minimum(wide, before(wide, 1))[:rows, 0:1]

    for copy in edges:
        copy.wait()
    speed_w = jnp.where(
        row_index((levels, cols)).astype(F32) < west_depth, from_west[1], 0.0
    )
    flux_west[...] = (
        jnp.maximum(speed_w, 0.0) * from_west[0] + jnp.minimum(speed_w, 0.0) * row_west[...]
    )
    speed_s = jnp.where(
        lane.astype(F32) < south_depth, pltpu.roll(from_south[...], HALF, 1), 0.0
    )
    flux_south[...] = (
        jnp.maximum(speed_s, 0.0) * from_south[...]
        + jnp.minimum(speed_s, 0.0) * col_south[...]
    )
    for at in range(chunks):
        loads[at][3].wait()

    last_row = row_index(tile) == rows - 1
    first_row = row_index(tile) == 0
    last_lane = lane_index(tile) == cols - 1
    first_lane = lane_index(tile) == 0

    def spread(side, shift):
        turned = pltpu.roll(side, shift, 1)
        return jnp.concatenate([turned] * (cols // LANES), axis=1)

    def forward(k, first):
        level = jnp.asarray(k, F32)
        here = temp[k]
        wet = level < depth[...]
        speed = jnp.where(level < depth_e[...], east[k], 0.0)
        there = jnp.where(last_row, from_east[pl.ds(k, 1), :], after(here, 0))
        flux = jnp.maximum(speed, 0.0) * here + jnp.minimum(speed, 0.0) * there
        total = flux - jnp.where(first_row, flux_west[pl.ds(k, 1), :], before(flux, 0))
        speed = jnp.where(level < depth_n[...], north[k], 0.0)
        there = jnp.where(
            last_lane, spread(from_north[...], LANES - 1 - k), after(here, 1)
        )
        flux = jnp.maximum(speed, 0.0) * here + jnp.minimum(speed, 0.0) * there
        total = total + (
            flux - jnp.where(first_lane, spread(flux_south[...], LANES - k), before(flux, 1))
        )
        numerator = here - advect_scale * jnp.where(wet, total, 0.0)
        below = jnp.where(
            level + 1.0 < depth[...], mix[jnp.minimum(k + 1, levels - 1)], 0.0
        )
        denominator = 1.0 + below
        if not first:
            above = jnp.where(wet, mix[k], 0.0)
            denominator = denominator + above * (1.0 - factor[k - 1])
            numerator = numerator + above * value[k - 1]
        scale = inverse_of(denominator)
        value[k] = numerator * scale
        factor[k] = below * scale

    forward(0, True)
    lax.fori_loop(1, levels, lambda k, c: (forward(k, False), c)[1], 0)

    def settle(k, x, tail, packed):
        temp_out[k] = x
        tail = tail + x
        half = tail - 0.5 * x
        factor[k] = half
        row_press[pl.ds(k, 1), :] = half[0:1, :]
        packed = jnp.where(lane == k, pltpu.roll(half[:, :LANES], k, 1), packed)
        return tail, packed

    def backward(step, carry):
        x, tail, packed = carry
        k = levels - 1 - step
        x = value[k] + factor[k] * x
        tail, packed = settle(k, x, tail, packed)
        return x, tail, packed

    x = value[levels - 1]
    tail, packed = settle(levels - 1, x, jnp.zeros(tile, F32), zero_side)
    x, tail, packed = lax.fori_loop(1, levels, backward, (x, tail, packed))
    surf_total = surf.at[0]
    surf_total[...] = tail
    row_press[...] = row_press[...] - tail[0:1, :]
    col_press[...] = packed - tail[:, 0:1]
    press = [
        send(row_press, press_east, edge_sems, 4, -1, 0),
        send(col_press, press_north, edge_sems, 5, 0, -1),
    ]
    for copy in press:
        copy.wait()

    totals_out[...] = jnp.zeros(totals_out.shape, F32)
    slope = force_scale / levels

    def momentum(k, carry):
        level = jnp.asarray(k, F32)
        here = factor[k] - surf[0]
        there = jnp.where(last_row, press_east[pl.ds(k, 1), :], after(here, 0))
        new = jnp.where(level < depth_e[...], east[k] + slope * (here - there), 0.0)
        speed_out[0, k] = new
        totals_out[0] += new
        there = jnp.where(
            last_lane, spread(press_north[...], LANES - 1 - k), after(here, 1)
        )
        new = jnp.where(level < depth_n[...], north[k] + slope * (here - there), 0.0)
        speed_out[1, k] = new
        totals_out[1] += new
        return carry

    lax.fori_loop(0, levels, momentum, 0)


def surface_kernel(
    levels, totals, root_in, inverse_in, source_in, out, bands, sides, corners, sems
):
    rows, cols = out.shape
    meet_neighbours()
    copies = start_halo(totals, bands, sides, corners, sems)
    for copy in copies:
        copy.wait()
    east = joined(0, totals, bands, sides, corners)
    north = joined(1, totals, bands, sides, corners)
    divergence = (east - before(east, 0) + north - before(north, 1)) * (1.0 / levels)
    root = root_in[...]
    inverse = inverse_in[...]
    forcing = jnp.where(root > 0.0, source_in[...] - divergence_scale * divergence, 0.0)
    scaled = forcing * inverse
    ratio = root * inverse
    update = scaled * (1.0 / cheb_gamma)
    iterate = update
    omega = 2.0 / cheb_gamma
    for _ in range(1, ITERS):
        omega = 1.0 / (cheb_gamma - omega / (4.0 * cheb_alpha * cheb_alpha))
        residual = scaled - iterate + ratio * around_total(root * iterate)
        update = omega * residual + (cheb_gamma * omega - 1.0) * update
        iterate = iterate + update
    out[...] = iterate[:rows, :cols]


def local(temp, speeds, mix, sea, tally, rain):
    levels, rows, cols = temp.shape
    wide = (rows + 2 * BAND, cols + LANES)
    vmem = pl.BlockSpec(memory_space=pltpu.VMEM)
    field = pltpu.VMEM((levels, rows, cols), F32)
    plane = pltpu.VMEM((rows, cols), F32)
    row_set = pltpu.VMEM((levels, cols), F32)
    col_set = pltpu.VMEM((rows, LANES), F32)
    temp_next, speed_next, totals, root, inverse, source = pl.pallas_call(
        columns_kernel,
        out_shape=[
            pltpu.VMEM((levels, rows, cols), F32),
            pltpu.VMEM((2, levels, rows, cols), F32),
            pltpu.VMEM((2, rows, cols), F32),
            pltpu.VMEM(wide, F32),
            pltpu.VMEM(wide, F32),
            pltpu.VMEM(wide, F32),
        ],
        in_specs=[pl.BlockSpec(memory_space=pltpu.HBM)] * 3 + [vmem] * 3,
        out_specs=[vmem] * 6,
        scratch_shapes=[field] * 6
        + [plane] * 3
        + [
            pltpu.VMEM((2, rows, cols), F32),
            pltpu.VMEM((2, levels, cols), F32),
            row_set,
            pltpu.VMEM((2, levels, cols), F32),
            row_set,
        ]
        + [col_set] * 4
        + [row_set, col_set]
        + [row_set, row_set, col_set, col_set]
        + [pltpu.SemaphoreType.DMA((levels // 8, 4)), pltpu.SemaphoreType.DMA((2, 6))]
        + halo_shapes(rows, cols),
        compiler_params=pltpu.CompilerParams(
            collective_id=0, has_side_effects=True, vmem_limit_bytes=30 * 2**20
        ),
        name="columns",
    )(temp, speeds, mix, sea, tally, rain)
    surface = pl.pallas_call(
        functools.partial(surface_kernel, levels),
        out_shape=jax.ShapeDtypeStruct((rows, cols), F32),
        in_specs=[vmem] * 4,
        out_specs=vmem,
        scratch_shapes=halo_shapes(rows, cols),
        compiler_params=pltpu.CompilerParams(
            collective_id=1, has_side_effects=True, vmem_limit_bytes=16 * 2**20
        ),
        name="surface",
    )(totals, root, inverse, source)
    return temp_next, speed_next, surface


def solution(mesh):
    tile = P("gx", "gy")
    column = P(None, "gx", "gy")
    pair = P(None, None, "gx", "gy")
    return jax.shard_map(
        local,
        mesh=mesh,
        in_specs=(column, pair, column, tile, tile, tile),
        out_specs=(column, pair, tile),
        check_vma=False,
    )
```

time: 207 us -> 55.5 us (0.27)
  other arithmetic: 87.3 us -> 0 us
  Pallas kernels: 0 us -> 41.5 us
  waiting for transfers between devices: 38.6 us -> 0 us
  local copies, waits for them, and re-layouts: 47.9 us -> 13 us
  starting transfers between devices: 31.1 us -> 0 us
    pallas_call x0 -> x2, Pallas kernels: none -> 41.5 us  [the longest x1 32.6 us: local(): pl.pallas_call(columns_kernel, out_shape=[pltpu.VMEM((levels, rows, cols)...]
    ppermute x32 -> x0, waiting for transfers between devices: 38.6 us -> none  [the longest x16 23.4 us: padded_2(): lax.ppermute(tail, axis, [(i, (i + 1) % count) for i in range(count)])]
    ppermute x32 -> x0, starting transfers between devices: 31.1 us -> none  [the longest x16 17.7 us: padded_2(): lax.ppermute(head, axis, [((i + 1) % count, i) for i in range(count)])]
    concatenate x15 -> x0, other arithmetic: 26.2 us -> none  [padded_2(): jnp.concatenate([lax.ppermute(tail, axis, [(i, (i + 1) % count) for i in...]
    slice x19 -> x0, local copies, waits for them, and re-layouts: 24.7 us -> none  [the longest x11 18.1 us: padded_2(): lax.slice_in_dim(cells, cells.shape[dim] - width, cells.shape[dim], axis=...]
    reduce_sum x2 -> x0, other arithmetic: 17.6 us -> none  [the longest x1 9.02 us: momentum_update(): north_total = jnp.sum(north_full, axis=0) / north_full.shape[0]]
    add x3 -> x0, other arithmetic: 11.4 us -> none  [the longest x1 5.52 us: tracer_update(): jnp.maximum(east_open, 0.0) * temp_ext[:, :-1, 1:-1]]
    ppermute x4 -> x0, local copies, waits for them, and re-layouts: 10.8 us -> none  [the longest x2 5.46 us: padded_2(): lax.ppermute(tail, axis, [(i, (i + 1) % count) for i in range(count)])]
  transfers between devices with their start and end apart: 32 -> 0, of which waited for: 21 -> 0; matrix products, arithmetic and copies ran while one was open for 44% -> 0% of each run, Pallas kernels for 0% -> 0%
where the time goes in v1:
time: 55.5 us; the launch traced here: 55.1 us
  Pallas kernels  41.5 us (75%)
  local copies, waits for them, and re-layouts  13 us (23%)
  between operations  0.66 us (1%)
    pallas_call x1, Pallas kernels, local(): pl.pallas_call(columns_kernel, out_shape=[pltpu.VMEM((levels, rows, cols)...  32.6 us
    unnamed x15, local copies, waits for them, and re-layouts  13 us
    pallas_call x1, Pallas kernels, local(): pl.pallas_call(functools.partial(surface_kernel, levels), out_shape=jax.S...  8.93 us

profile of v1, /device:TPU:0, one launch (start us, length us, event | category | flops | bytes accessed | tf_op | source)
XLA Modules:
  0.0 55.1 jit_solution(7065210084250576947)
XLA Ops:
  0.6 0.0 copy-start
  0.6 2.5 %copy-done = f32[2,40,64,256]{3,2,1,0:T(8,128)S(1)} copy-done((f32[2,40,64,256]{3,2,1,0:T(8,128)S(1)}, f32[2,40,64,256]{3,2,1,0:T(8,128)}, u32[]{:S(2)}) %copy-start) | copy-done | bytes 5242904
  3.1 0.0 copy-start.1
  3.1 1.7 %copy-done.1 = f32[40,64,256]{2,1,0:T(8,128)S(1)} copy-done((f32[40,64,256]{2,1,0:T(8,128)S(1)}, f32[40,64,256]{2,1,0:T(8,128)}, u32[]{:S(2)}) %copy-start.1) | copy-done | bytes 2621464
  4.9 0.0 copy-start.2
  4.9 1.7 %copy-done.2 = f32[40,64,256]{2,1,0:T(8,128)S(1)} copy-done((f32[40,64,256]{2,1,0:T(8,128)S(1)}, f32[40,64,256]{2,1,0:T(8,128)}, u32[]{:S(2)}) %copy-start.2) | copy-done | bytes 2621464
  6.6 0.0 copy-start.3
  6.6 0.8 %copy-done.3 = s32[64,256]{1,0:T(8,128)S(1)} copy-done((s32[64,256]{1,0:T(8,128)S(1)}, s32[64,256]{1,0:T(8,128)}, u32[]{:S(2)}) %copy-start.3) | copy-done | bytes 65560
  7.4 0.0 copy-start.4
  7.4 0.8 %copy-done.4 = s32[64,256]{1,0:T(8,128)S(1)} copy-done((s32[64,256]{1,0:T(8,128)S(1)}, s32[64,256]{1,0:T(8,128)}, u32[]{:S(2)}) %copy-start.4) | copy-done | bytes 65560
  8.3 0.0 copy-start.5
  8.3 0.8 %copy-done.5 = f32[64,256]{1,0:T(8,128)S(1)} copy-done((f32[64,256]{1,0:T(8,128)S(1)}, f32[64,256]{1,0:T(8,128)}, u32[]{:S(2)}) %copy-start.5) | copy-done | bytes 65560
  9.1 32.6 %columns.1 = (f32[40,64,256]{2,1,0:T(8,128)S(1)}, f32[2,40,64,256]{3,2,1,0:T(8,128)S(1)}, f32[2,64,256]{2,1,0:T(8,128)S(1)}, f32[80,384]{1,0:T(8,128)S(1)}, f32[...) custom-call(f32[40,64,256]{2,1,0:T(8,128)S(1)} %copy-done.1, f32[2,40,64,256]{3,2,1,0:T(8,128)S(1)} %copy-done, ...), custom_call_target="tpu_custom_call" | custom-call | tf_op jit(solution)/shard_map/columns/pallas_call | solution.py:390
  41.7 1.5 %copy.12 = f32[40,64,256]{2,1,0:T(8,128)} copy(f32[40,64,256]{2,1,0:T(8,128)S(1)} %get-tuple-element.15) | data formatting | bytes 5242880
  43.2 8.9 %surface.1 = f32[64,256]{1,0:T(8,128)S(1)} custom-call(f32[2,64,256]{2,1,0:T(8,128)S(1)} %get-tuple-element.11.totals, f32[80,384]{1,0:T(8,128)S(1)} %get-tuple-element.12.root_in, f32[80,384]{1,0:T(8,128)S(1)} %get-tuple-element.13.inverse_in, f32[80,384]{1,0:T(8,128)S(1)} %get-tuple-element.14.source_in), custom_call_target="tpu_custom_call" | custom-call | tf_op jit(solution)/shard_map/surface/pallas_call | solution.py:421
  52.1 2.4 %copy.13 = f32[2,40,64,256]{3,2,1,0:T(8,128)} copy(f32[2,40,64,256]{3,2,1,0:T(8,128)S(1)} %get-tuple-element.16) | data formatting | bytes 10485760
  54.5 0.6 %copy.14 = f32[64,256]{1,0:T(8,128)} copy(f32[64,256]{1,0:T(8,128)S(1)} %surface.1) | data formatting | bytes 131072
Async XLA Ops:
  0.6 2.5 %copy-start = (f32[2,40,64,256]{3,2,1,0:T(8,128)S(1)}, f32[2,40,64,256]{3,2,1,0:T(8,128)}, u32[]{:S(2)}) copy-start(f32[2,40,64,256]{3,2,1,0:T(8,128)} %speed_hbm.1) | copy-start | bytes 15728644
  3.1 1.7 %copy-start.1 = (f32[40,64,256]{2,1,0:T(8,128)S(1)}, f32[40,64,256]{2,1,0:T(8,128)}, u32[]{:S(2)}) copy-start(f32[40,64,256]{2,1,0:T(8,128)} %temp_hbm.1) | copy-start | bytes 7864324
  4.9 1.7 %copy-start.2 = (f32[40,64,256]{2,1,0:T(8,128)S(1)}, f32[40,64,256]{2,1,0:T(8,128)}, u32[]{:S(2)}) copy-start(f32[40,64,256]{2,1,0:T(8,128)} %mix_hbm.1) | copy-start | bytes 7864324
  6.6 0.8 %copy-start.3 = (s32[64,256]{1,0:T(8,128)S(1)}, s32[64,256]{1,0:T(8,128)}, u32[]{:S(2)}) copy-start(s32[64,256]{1,0:T(8,128)} %sea.1) | copy-start | bytes 196612
  7.4 0.8 %copy-start.4 = (s32[64,256]{1,0:T(8,128)S(1)}, s32[64,256]{1,0:T(8,128)}, u32[]{:S(2)}) copy-start(s32[64,256]{1,0:T(8,128)} %tally.1) | copy-start | bytes 196612
  8.3 0.8 %copy-start.5 = (f32[64,256]{1,0:T(8,128)S(1)}, f32[64,256]{1,0:T(8,128)}, u32[]{:S(2)}) copy-start(f32[64,256]{1,0:T(8,128)} %rain.1) | copy-start | bytes 196612

commit v2 on v1

v2 whole, which is shorter than its diff:
```python
import jax
import jax.numpy as jnp
from jax import lax
from jax.experimental import pallas as pl
from jax.experimental.pallas import tpu as pltpu
from jax.sharding import PartitionSpec as P

ITERS = 6
damping = 0.05
lower_bound = 0.02
upper_bound = 2.0
cheb_alpha = 2.0 / (upper_bound - lower_bound)
cheb_gamma = (upper_bound + lower_bound) / 2.0
advect_scale = 0.4
force_scale = 4.0
source_scale = 0.5
divergence_scale = 4.0

MESH = pl.DeviceIdType.MESH
LANES = 128
HALF = LANES // 2
GROUP = 8
BAND = 8
F32 = jnp.float32
AROUND = ((1, 0), (-1, 0), (0, 1), (0, -1), (1, 1), (1, -1), (-1, 1), (-1, -1))


def device_at(dx, dy):
    nx, ny = lax.axis_size("gx"), lax.axis_size("gy")
    return (
        lax.rem(lax.axis_index("gx") + (dx + nx), nx),
        lax.rem(lax.axis_index("gy") + (dy + ny), ny),
    )


def meet_neighbours():
    barrier = pltpu.get_barrier_semaphore()
    for dx, dy in AROUND:
        pl.semaphore_signal(barrier, inc=1, device_id=device_at(dx, dy), device_id_type=MESH)
    pl.semaphore_wait(barrier, len(AROUND))


def send(src, dst, sems, at, dx, dy):
    copy = pltpu.make_async_remote_copy(
        src_ref=src,
        dst_ref=dst,
        send_sem=sems.at[0, at],
        recv_sem=sems.at[1, at],
        device_id=device_at(dx, dy),
        device_id_type=MESH,
    )
    copy.start()
    return copy


def halo_shapes(rows, cols):
    return [
        pltpu.VMEM((2, 2, BAND, cols), F32),
        pltpu.VMEM((2, 2, rows, LANES), F32),
        pltpu.VMEM((4, 2, BAND, LANES), F32),
        pltpu.SemaphoreType.DMA((2, 8)),
    ]


def start_halo(pair, bands, sides, corners, sems):
    rows, cols = pair.shape[1:]
    low, high = pl.ds(0, BAND), pl.ds(rows - BAND, BAND)
    left, right = pl.ds(0, LANES), pl.ds(cols - LANES, LANES)
    return [
        send(pair.at[:, low, :], bands.at[0], sems, 0, -1, 0),
        send(pair.at[:, high, :], bands.at[1], sems, 1, 1, 0),
        send(pair.at[:, :, left], sides.at[0], sems, 2, 0, -1),
        send(pair.at[:, :, right], sides.at[1], sems, 3, 0, 1),
        send(pair.at[:, low, left], corners.at[0], sems, 4, -1, -1),
        send(pair.at[:, low, right], corners.at[1], sems, 5, -1, 1),
        send(pair.at[:, high, left], corners.at[2], sems, 6, 1, -1),
        send(pair.at[:, high, right], corners.at[3], sems, 7, 1, 1),
    ]


def lane_index(shape):
    return lax.broadcasted_iota(jnp.int32, shape, len(shape) - 1)


def row_index(shape):
    return lax.broadcasted_iota(jnp.int32, shape, len(shape) - 2)


def joined(which, pair, bands, sides, corners):
    def lanes(own, north, south):
        return jnp.concatenate(
            [own, jnp.where(lane_index(north.shape) < HALF, north, south)], axis=1
        )

    return jnp.concatenate(
        [
            lanes(pair[which], sides[0, which], sides[1, which]),
            lanes(bands[0, which], corners[0, which], corners[1, which]),
            lanes(bands[1, which], corners[2, which], corners[3, which]),
        ],
        axis=0,
    )


def after(field, axis):
    return pltpu.roll(field, field.shape[axis] - 1, axis)


def before(field, axis):
    return pltpu.roll(field, 1, axis)


def around_total(field):
    pair = after(field, 0) + before(field, 0)
    slanted = field + 0.5 * pair
    return pair + after(slanted, 1) + before(slanted, 1)


def inverse_of(value):
    near = pl.reciprocal(value, approx=True)
    return near * (2.0 - value * near)


def fill(k, packed, lane, side, shift):
    return jnp.where(lane == k, pltpu.roll(side, shift, 1), packed)


def by_level(levels, body, carry):
    def step(at, carry):
        for inner in range(GROUP):
            carry = body(at * GROUP + inner, carry)
        return carry

    return lax.fori_loop(0, levels // GROUP, step, carry)


def columns_kernel(
    temp_hbm,
    speed_hbm,
    mix_hbm,
    sea_hbm,
    tally_hbm,
    rain_hbm,
    temp_out,
    speed_out,
    root_out,
    ratio_out,
    scaled_out,
    temp,
    east,
    north,
    mix,
    value,
    factor,
    scale,
    sea,
    tally,
    depth,
    depth_e,
    depth_n,
    surf,
    totals,
    tail_ref,
    row_east,
    row_west,
    from_west,
    from_east,
    col_north,
    col_south,
    from_south,
    from_north,
    press_row,
    press_from_east,
    press_col,
    press_from_north,
    fix_row,
    fix_col,
    load_sems,
    edge_sems,
    bands,
    sides,
    corners,
    halo_sems,
    total_bands,
    total_sides,
    total_corners,
    total_sems,
):
    levels, rows, cols = temp.shape
    strips = rows // BAND
    pairs = [
        (sea_hbm, sea),
        (tally_hbm, tally),
        (rain_hbm, surf.at[1]),
        (temp_hbm, temp),
        (speed_hbm.at[0], east),
        (speed_hbm.at[1], north),
        (mix_hbm, mix.at[pl.ds(0, levels)]),
    ]
    loads = [
        pltpu.make_async_copy(src, dst, load_sems.at[at]) for at, (src, dst) in enumerate(pairs)
    ]
    for copy in loads:
        copy.start()
    meet_neighbours()
    for copy in loads[:3]:
        copy.wait()

    tile = (rows, cols)
    latitude = lax.axis_index("gy") * cols + lane_index(tile)
    inner = (latitude > 0) & (latitude < cols * lax.axis_size("gy") - 1)
    wet_levels = jnp.where(inner & (sea[...] == 1), tally[...], 0).astype(F32)
    depth[...] = wet_levels
    surf[0] = wet_levels
    surf_copies = start_halo(surf, bands, sides, corners, halo_sems)

    lane = lane_index((rows, LANES))
    zero_side = jnp.zeros((rows, LANES), F32)
    low, high = slice(0, LANES), slice(cols - LANES, cols)
    mix[levels] = jnp.zeros(tile, F32)

    def pack_temp(k, carry):
        to_north, to_south = carry
        one = pl.ds(k, 1)
        row_east[0, one, :] = temp[k, rows - 1 : rows, :]
        row_west[one, :] = temp[k, 0:1, :]
        to_north = fill(k, to_north, lane, temp[k, :, high], k + 1)
        to_south = fill(k, to_south, lane, temp[k, :, low], k)
        return to_north, to_south

    def pack_speed(k, to_north):
        row_east[1, pl.ds(k, 1), :] = east[k, rows - 1 : rows, :]
        return fill(k + HALF, to_north, lane, north[k, :, high], k + 1 + HALF)

    loads[3].wait()
    to_north, to_south = by_level(levels, pack_temp, (zero_side, zero_side))
    col_south[...] = to_south
    edges = [
        send(row_west, from_east, edge_sems, 0, -1, 0),
        send(col_south, from_north, edge_sems, 1, 0, -1),
    ]
    loads[4].wait()
    loads[5].wait()
    col_north[...] = by_level(levels, pack_speed, to_north)
    edges += [
        send(row_east, from_west, edge_sems, 2, 1, 0),
        send(col_north, from_south, edge_sems, 3, 0, 1),
    ]

    for copy in surf_copies:
        copy.wait()
    wide = joined(0, surf, bands, sides, corners)
    source = source_scale * joined(1, surf, bands, sides, corners)
    root = jnp.sqrt(wide / levels)
    inverse = 1.0 / (damping + root * around_total(root))
    root_out[...] = root
    ratio_out[...] = root * inverse
    scaled_out[...] = jnp.where(root > 0.0, source * inverse, 0.0)
    open_e = jnp.minimum(wide, after(wide, 0))[:rows, :cols]
    open_n = jnp.minimum(wide, after(wide, 1))[:rows, :cols]
    open_w = jnp.minimum(wide, before(wide, 0))[0:1, :cols]
    open_s = jnp.minimum(wide, before(wide, 1))[:rows, 0:1]
    last_e = open_e[rows - 1 : rows, :]
    last_n = open_n[:, cols - 1 : cols]
    depth_e[...] = jnp.where(row_index(tile) == rows - 1, 0.0, open_e)
    depth_n[...] = jnp.where(lane_index(tile) == cols - 1, 0.0, open_n)
    loads[6].wait()

    band = (BAND, cols)
    band_row = row_index(band)

    def upwind(open_depth, level, speed, here, there):
        flux = speed * jnp.where(speed > 0.0, here, there)
        return jnp.where(level < open_depth, flux, 0.0)

    def assemble(k, carry):
        level = jnp.asarray(k, F32)
        part = [pl.ds(at * BAND, BAND) for at in range(strips)]
        previous = jnp.zeros(band, F32)
        here = temp[k, part[0], :]
        turned = pltpu.roll(here, BAND - 1, 0)
        for at in range(strips):
            if at + 1 < strips:
                later = temp[k, part[at + 1], :]
                later_turned = pltpu.roll(later, BAND - 1, 0)
                there = jnp.where(band_row == BAND - 1, later_turned, turned)
            else:
                there = turned
            flux = upwind(depth_e[part[at], :], level, east[k, part[at], :], here, there)
            turned_flux = pltpu.roll(flux, 1, 0)
            total = flux - jnp.where(band_row == 0, previous, turned_flux)
            previous = turned_flux
            flux = upwind(
                depth_n[part[at], :], level, north[k, part[at], :], here, after(here, 1)
            )
            total = total + (flux - before(flux, 1))
            value[k, part[at], :] = here - advect_scale * total
            above = mix[k, part[at], :]
            below = jnp.where(level + 1.0 < depth[part[at], :], mix[k + 1, part[at], :], 0.0)
            mix[k + 1, part[at], :] = below
            inverse_pivot = inverse_of(
                (1.0 + below) + above * (1.0 - factor[jnp.maximum(k - 1, 0), part[at], :])
            )
            scale[k, part[at], :] = inverse_pivot
            factor[k, part[at], :] = below * inverse_pivot
            if at + 1 < strips:
                here, turned = later, later_turned
        return carry

    mix[0] = jnp.zeros(tile, F32)
    factor[0] = jnp.zeros(tile, F32)
    lax.fori_loop(0, levels, assemble, 0)

    for copy in edges:
        copy.wait()
    level_row = row_index((levels, cols)).astype(F32)
    level_lane = lane.astype(F32)
    flux_w = upwind(open_w, level_row, from_west[1], from_west[0], row_west[...])
    flux_e = upwind(last_e, level_row, row_east[1], row_east[0], from_east[...])
    flux_s = upwind(
        open_s, level_lane, pltpu.roll(from_south[...], HALF, 1), from_south[...], col_south[...]
    )
    flux_n = upwind(
        last_n, level_lane, pltpu.roll(col_north[...], HALF, 1), col_north[...], from_north[...]
    )
    from_west[0] = advect_scale * flux_w
    from_west[1] = advect_scale * flux_e
    from_south[...] = advect_scale * flux_s
    from_north[...] = advect_scale * flux_n

    def add_rim(k, carry):
        one = pl.ds(k, 1)
        value[k, 0:1, :] += from_west[0, one, :]
        value[k, rows - 1 : rows, :] -= from_west[1, one, :]
        value[k, :, low] += jnp.where(lane == 0, pltpu.roll(from_south[...], LANES - k, 1), 0.0)
        value[k, :, high] -= jnp.where(
            lane == LANES - 1, pltpu.roll(from_north[...], LANES - 1 - k, 1), 0.0
        )
        return carry

    by_level(levels, add_rim, 0)

    def forward(k, x):
        x = (value[k] + mix[k] * x) * scale[k]
        value[k] = x
        return x

    x = by_level(levels, forward, jnp.zeros(tile, F32))

    slope = force_scale / levels

    def backward(step, carry):
        x, tail = carry
        k = levels - 1 - step
        x = value[k] + factor[k] * x
        temp_out[k] = x
        part = slope * x
        tail = tail + part
        factor[k] = tail - 0.5 * part
        return x, tail

    x, tail = by_level(levels, backward, (jnp.zeros(tile, F32), jnp.zeros(tile, F32)))
    tail_ref[...] = tail

    def pack_press(k, carry):
        to_north, to_south = carry
        one = pl.ds(k, 1)
        press_row[0, one, :] = factor[k, 0:1, :]
        press_row[1, one, :] = factor[k, rows - 1 : rows, :]
        to_north = fill(k, to_north, lane, factor[k, :, high], k + 1)
        to_south = fill(k, to_south, lane, factor[k, :, low], k)
        return to_north, to_south

    to_north, to_south = by_level(levels, pack_press, (zero_side, zero_side))
    press_row[0] -= tail[0:1, :]
    press_row[1] -= tail[rows - 1 : rows, :]
    press_col[0] = to_south - tail[:, 0:1]
    press_col[1] = to_north - tail[:, cols - 1 : cols]
    press = [
        send(press_row.at[0], press_from_east, edge_sems, 4, -1, 0),
        send(press_col.at[0], press_from_north, edge_sems, 5, 0, -1),
    ]

    totals[...] = jnp.zeros(totals.shape, F32)

    def momentum(k, carry):
        level = jnp.asarray(k, F32)
        part = [pl.ds(at * BAND, BAND) for at in range(strips)]
        here = factor[k, part[0], :] - tail_ref[part[0], :]
        turned = pltpu.roll(here, BAND - 1, 0)
        for at in range(strips):
            if at + 1 < strips:
                later = factor[k, part[at + 1], :] - tail_ref[part[at + 1], :]
                later_turned = pltpu.roll(later, BAND - 1, 0)
                there = jnp.where(band_row == BAND - 1, later_turned, turned)
            else:
                there = turned
            speed = east[k, part[at], :] + (here - there)
            speed = jnp.where(level < depth_e[part[at], :], speed, 0.0)
            speed_out[0, k, part[at], :] = speed
            totals[0, part[at], :] += speed
            speed = north[k, part[at], :] + (here - after(here, 1))
            speed = jnp.where(level < depth_n[part[at], :], speed, 0.0)
            speed_out[1, k, part[at], :] = speed
            totals[1, part[at], :] += speed
            if at + 1 < strips:
                here, turned = later, later_turned
        return carry

    lax.fori_loop(0, levels, momentum, 0)

    for copy in press:
        copy.wait()
    speed_e = row_east[1] + (press_row[1] - press_from_east[...])
    speed_e = jnp.where(level_row < last_e, speed_e, 0.0)
    speed_n = pltpu.roll(col_north[...], HALF, 1) + (press_col[1] - press_from_north[...])
    speed_n = jnp.where(level_lane < last_n, speed_n, 0.0)
    fix_row[...] = speed_e
    fix_col[...] = speed_n
    totals[0, rows - 1 : rows, :] = jnp.sum(speed_e, axis=0, keepdims=True)
    totals[1, :, high] += jnp.where(
        lane == LANES - 1, jnp.sum(speed_n, axis=1, keepdims=True), 0.0
    )
    total_copies = start_halo(totals, total_bands, total_sides, total_corners, total_sems)

    def add_last(k, carry):
        speed_out[0, k, rows - 1 : rows, :] = fix_row[pl.ds(k, 1), :]
        speed_out[1, k, :, high] += jnp.where(
            lane == LANES - 1, pltpu.roll(fix_col[...], LANES - 1 - k, 1), 0.0
        )
        return carry

    by_level(levels, add_last, 0)

    for copy in total_copies:
        copy.wait()
    total_e = joined(0, totals, total_bands, total_sides, total_corners)
    total_n = joined(1, totals, total_bands, total_sides, total_corners)
    divergence = total_e - before(total_e, 0) + total_n - before(total_n, 1)
    root = root_out[...]
    inverse = 1.0 / (damping + root * around_total(root))
    scaled_out[...] -= jnp.where(
        root > 0.0, inverse * ((divergence_scale / levels) * divergence), 0.0
    )


def surface_kernel(
    temp_in, speed_in, root_in, ratio_in, scaled_in, temp_out, speed_out, out, sems
):
    rows, cols = out.shape
    copies = [
        pltpu.make_async_copy(temp_in, temp_out, sems.at[0]),
        pltpu.make_async_copy(speed_in.at[0], speed_out.at[0], sems.at[1]),
        pltpu.make_async_copy(speed_in.at[1], speed_out.at[1], sems.at[2]),
    ]
    for copy in copies:
        copy.start()
    root = root_in[...]
    ratio = ratio_in[...]
    scaled = scaled_in[...]
    update = scaled * (1.0 / cheb_gamma)
    iterate = update
    omega = 2.0 / cheb_gamma
    for _ in range(1, ITERS):
        omega = 1.0 / (cheb_gamma - omega / (4.0 * cheb_alpha * cheb_alpha))
        residual = scaled - iterate + ratio * around_total(root * iterate)
        update = omega * residual + (cheb_gamma * omega - 1.0) * update
        iterate = iterate + update
    out[...] = iterate[:rows, :cols]
    for copy in copies:
        copy.wait()


def local(temp, speeds, mix, sea, tally, rain):
    levels, rows, cols = temp.shape
    wide = pltpu.VMEM((rows + 2 * BAND, cols + LANES), F32)
    vmem = pl.BlockSpec(memory_space=pltpu.VMEM)
    field = pltpu.VMEM((levels, rows, cols), F32)
    plane = pltpu.VMEM((rows, cols), F32)
    plane_int = pltpu.VMEM((rows, cols), jnp.int32)
    two_planes = pltpu.VMEM((2, rows, cols), F32)
    row_set = pltpu.VMEM((levels, cols), F32)
    row_sets = pltpu.VMEM((2, levels, cols), F32)
    col_set = pltpu.VMEM((rows, LANES), F32)
    col_sets = pltpu.VMEM((2, rows, LANES), F32)
    inputs = [
        pltpu.with_memory_space_constraint(array, pltpu.HBM)
        for array in (temp, speeds, mix, sea, tally, rain)
    ]
    temp_next, speed_next, root, ratio, scaled = pl.pallas_call(
        columns_kernel,
        out_shape=[field, pltpu.VMEM((2, levels, rows, cols), F32), wide, wide, wide],
        in_specs=[pl.BlockSpec(memory_space=pltpu.HBM)] * 6,
        out_specs=[vmem] * 5,
        scratch_shapes=[field] * 3
        + [pltpu.VMEM((levels + 1, rows, cols), F32)]
        + [field] * 3
        + [plane_int] * 2
        + [plane] * 3
        + [two_planes, two_planes, plane]
        + [row_sets, row_set, row_sets, row_set]
        + [col_set] * 4
        + [row_sets, row_set, col_sets, col_set]
        + [row_set, col_set]
        + [pltpu.SemaphoreType.DMA((7,)), pltpu.SemaphoreType.DMA((2, 6))]
        + halo_shapes(rows, cols) * 2,
        compiler_params=pltpu.CompilerParams(
            collective_id=0, has_side_effects=True, vmem_limit_bytes=48 * 2**20
        ),
        name="columns",
    )(*inputs)
    return pl.pallas_call(
        surface_kernel,
        out_shape=[
            jax.ShapeDtypeStruct(temp.shape, F32),
            jax.ShapeDtypeStruct(speeds.shape, F32),
            jax.ShapeDtypeStruct((rows, cols), F32),
        ],
        in_specs=[vmem] * 5,
        out_specs=[pl.BlockSpec(memory_space=pltpu.HBM)] * 2 + [vmem],
        scratch_shapes=[pltpu.SemaphoreType.DMA((3,))],
        compiler_params=pltpu.CompilerParams(vmem_limit_bytes=48 * 2**20),
        name="surface",
    )(temp_next, speed_next, root, ratio, scaled)


def solution(mesh):
    tile = P("gx", "gy")
    column = P(None, "gx", "gy")
    pair = P(None, None, "gx", "gy")
    return jax.shard_map(
        local,
        mesh=mesh,
        in_specs=(column, pair, column, tile, tile, tile),
        out_specs=(column, pair, tile),
        check_vma=False,
    )
```

time: 55.5 us -> 41.3 us (0.74)
  local copies, waits for them, and re-layouts: 13 us -> 2.29 us
  Pallas kernels: 41.5 us -> 38.2 us
    unnamed x15 -> x2, local copies, waits for them, and re-layouts: 13 us -> 2.29 us
    pallas_call x2, Pallas kernels: 41.5 us -> 38.2 us  [the longest x1 31.8 us: local(): pl.pallas_call(columns_kernel, out_shape=[field, pltpu.VMEM((2, levels, r...]
where the time goes in v2:
time: 41.3 us; the launch traced here: 41.1 us
  Pallas kernels  38.2 us (92%)
  local copies, waits for them, and re-layouts  2.29 us (6%)
  between operations  0.65 us (2%)
    pallas_call x1, Pallas kernels, local(): pl.pallas_call(columns_kernel, out_shape=[field, pltpu.VMEM((2, levels, r...  31.8 us
    pallas_call x1, Pallas kernels, local(): pl.pallas_call(surface_kernel, out_shape=[jax.ShapeDtypeStruct(temp.shape...  6.36 us
    unnamed x2, local copies, waits for them, and re-layouts  2.29 us

profile of v2, /device:TPU:0, one launch (start us, length us, event | category | flops | bytes accessed | tf_op | source)
XLA Modules:
  0.0 41.1 jit_solution(16958557727560878798)
XLA Ops:
  0.6 31.8 %columns.1 = (f32[40,64,256]{2,1,0:T(8,128)S(1)}, f32[2,40,64,256]{3,2,1,0:T(8,128)S(1)}, f32[80,384]{1,0:T(8,128)S(1)}, f32[80,384]{1,0:T(8,128)S(1)}, f32[80,384]{1,0:T(8,128)S(1)}) custom-call(f32[40,64,256]{2,1,0:T(8,128)} %temp_hbm.1, f32[2,40,64,256]{3,2,1,0:T(8,128)} %speed_hbm.1, f32[40,64,256]{2,1,0:T(8,128)} %mix_hbm.1, s32[64,256]{1,0:T(8,128)} %sea_hbm.1, ...), custom_call_target="tpu_custom_call" | custom-call | tf_op jit(solution)/shard_map/columns/pallas_call | solution.py:490
  32.4 0.0 copy-start
  32.5 2.3 %copy-done = f32[2,40,64,256]{3,2,1,0:T(8,128)} copy-done((f32[2,40,64,256]{3,2,1,0:T(8,128)}, f32[2,40,64,256]{3,2,1,0:T(8,128)S(1)}, u32[]{:S(2)}) %copy-start) | copy-done | bytes 5242904
  34.7 6.4 %surface.1 = (f32[40,64,256]{2,1,0:T(8,128)}, f32[2,40,64,256]{3,2,1,0:T(8,128)}, f32[64,256]{1,0:T(8,128)}) custom-call(f32[40,64,256]{2,1,0:T(8,128)S(1)} %get-tuple-element.8.temp_in, f32[2,40,64,256]{3,2,1,0:T(8,128)} %copy-done, f32[80,384]{1,0:T(8,128)S(1)} %get-tuple-element.10.root_in, f32[80,384]{1,0:T(8,128)S(1)} %get-tuple-element.11.ratio_in, ...), custom_call_target="tpu_custom_call" | custom-call | tf_op jit(solution)/shard_map/surface/pallas_call | solution.py:512
Async XLA Ops:
  32.4 2.3 %copy-start = (f32[2,40,64,256]{3,2,1,0:T(8,128)}, f32[2,40,64,256]{3,2,1,0:T(8,128)S(1)}, u32[]{:S(2)}) copy-start(f32[2,40,64,256]{3,2,1,0:T(8,128)S(1)} %get-tuple-element.9.speed_in) | copy-start | bytes 15728644

commit v3 on v2

--- a/solution.py
+++ b/solution.py
@@ -33,11 +33,18 @@
     )
 
 
+def greet_neighbours():
+    for dx, dy in AROUND:
+        pl.semaphore_signal(
+            pltpu.get_barrier_semaphore(),
+            inc=1,
+            device_id=device_at(dx, dy),
+            device_id_type=MESH,
+        )
+
+
 def meet_neighbours():
-    barrier = pltpu.get_barrier_semaphore()
-    for dx, dy in AROUND:
-        pl.semaphore_signal(barrier, inc=1, device_id=device_at(dx, dy), device_id_type=MESH)
-    pl.semaphore_wait(barrier, len(AROUND))
+    pl.semaphore_wait(pltpu.get_barrier_semaphore(), len(AROUND))
 
 
 def send(src, dst, sems, at, dx, dy):
@@ -153,6 +160,7 @@
     value,
     factor,
     scale,
+    coupling,
     sea,
     tally,
     depth,
@@ -188,6 +196,7 @@
 ):
     levels, rows, cols = temp.shape
     strips = rows // BAND
+    greet_neighbours()
     pairs = [
         (sea_hbm, sea),
         (tally_hbm, tally),
@@ -195,14 +204,13 @@
         (temp_hbm, temp),
         (speed_hbm.at[0], east),
         (speed_hbm.at[1], north),
-        (mix_hbm, mix.at[pl.ds(0, levels)]),
+        (mix_hbm, mix),
     ]
     loads = [
         pltpu.make_async_copy(src, dst, load_sems.at[at]) for at, (src, dst) in enumerate(pairs)
     ]
     for copy in loads:
         copy.start()
-    meet_neighbours()
     for copy in loads[:3]:
         copy.wait()
 
@@ -212,13 +220,16 @@
     wet_levels = jnp.where(inner & (sea[...] == 1), tally[...], 0).astype(F32)
     depth[...] = wet_levels
     surf[0] = wet_levels
-    surf_copies = start_halo(surf, bands, sides, corners, halo_sems)
+    depth_e[...] = jnp.where(
+        row_index(tile) == rows - 1, 0.0, jnp.minimum(wet_levels, after(wet_levels, 0))
+    )
+    depth_n[...] = jnp.where(
+        lane_index(tile) == cols - 1, 0.0, jnp.minimum(wet_levels, after(wet_levels, 1))
+    )
 
     lane = lane_index((rows, LANES))
     zero_side = jnp.zeros((rows, LANES), F32)
     low, high = slice(0, LANES), slice(cols - LANES, cols)
-    mix[levels] = jnp.zeros(tile, F32)
-
     def pack_temp(k, carry):
         to_north, to_south = carry
         one = pl.ds(k, 1)
@@ -235,6 +246,8 @@
     loads[3].wait()
     to_north, to_south = by_level(levels, pack_temp, (zero_side, zero_side))
     col_south[...] = to_south
+    meet_neighbours()
+    surf_copies = start_halo(surf, bands, sides, corners, halo_sems)
     edges = [
         send(row_west, from_east, edge_sems, 0, -1, 0),
         send(col_south, from_north, edge_sems, 1, 0, -1),
@@ -247,23 +260,6 @@
         send(col_north, from_south, edge_sems, 3, 0, 1),
     ]
 
-    for copy in surf_copies:
-        copy.wait()
-    wide = joined(0, surf, bands, sides, corners)
-    source = source_scale * joined(1, surf, bands, sides, corners)
-    root = jnp.sqrt(wide / levels)
-    inverse = 1.0 / (damping + root * around_total(root))
-    root_out[...] = root
-    ratio_out[...] = root * inverse
-    scaled_out[...] = jnp.where(root > 0.0, source * inverse, 0.0)
-    open_e = jnp.minimum(wide, after(wide, 0))[:rows, :cols]
-    open_n = jnp.minimum(wide, after(wide, 1))[:rows, :cols]
-    open_w = jnp.minimum(wide, before(wide, 0))[0:1, :cols]
-    open_s = jnp.minimum(wide, before(wide, 1))[:rows, 0:1]
-    last_e = open_e[rows - 1 : rows, :]
-    last_n = open_n[:, cols - 1 : cols]
-    depth_e[...] = jnp.where(row_index(tile) == rows - 1, 0.0, open_e)
-    depth_n[...] = jnp.where(lane_index(tile) == cols - 1, 0.0, open_n)
     loads[6].wait()
 
     band = (BAND, cols)
@@ -273,13 +269,17 @@
         flux = speed * jnp.where(speed > 0.0, here, there)
         return jnp.where(level < open_depth, flux, 0.0)
 
+    part = [pl.ds(at * BAND, BAND) for at in range(strips)]
+
     def assemble(k, carry):
         level = jnp.asarray(k, F32)
-        part = [pl.ds(at * BAND, BAND) for at in range(strips)]
+        later_level = jnp.minimum(k + 1, levels - 1)
+        result = []
         previous = jnp.zeros(band, F32)
         here = temp[k, part[0], :]
         turned = pltpu.roll(here, BAND - 1, 0)
         for at in range(strips):
+            above, keep = carry[at]
             if at + 1 < strips:
                 later = temp[k, part[at + 1], :]
                 later_turned = pltpu.roll(later, BAND - 1, 0)
@@ -295,21 +295,29 @@
             )
             total = total + (flux - before(flux, 1))
             value[k, part[at], :] = here - advect_scale * total
-            above = mix[k, part[at], :]
-            below = jnp.where(level + 1.0 < depth[part[at], :], mix[k + 1, part[at], :], 0.0)
-            mix[k + 1, part[at], :] = below
-            inverse_pivot = inverse_of(
-                (1.0 + below) + above * (1.0 - factor[jnp.maximum(k - 1, 0), part[at], :])
+            coupling[k, part[at], :] = above
+            below = jnp.where(
+                level + 1.0 < depth[part[at], :], mix[later_level, part[at], :], 0.0
             )
+            inverse_pivot = inverse_of((1.0 + below) + above * keep)
             scale[k, part[at], :] = inverse_pivot
-            factor[k, part[at], :] = below * inverse_pivot
+            leading = below * inverse_pivot
+            factor[k, part[at], :] = leading
+            result.append((below, 1.0 - leading))
             if at + 1 < strips:
                 here, turned = later, later_turned
-        return carry
-
-    mix[0] = jnp.zeros(tile, F32)
-    factor[0] = jnp.zeros(tile, F32)
-    lax.fori_loop(0, levels, assemble, 0)
+        return tuple(result)
+
+    nothing = jnp.zeros(band, F32)
+    lax.fori_loop(0, levels, assemble, ((nothing, nothing),) * strips)
+
+    for copy in surf_copies:
+        copy.wait()
+    wide = joined(0, surf, bands, sides, corners)
+    last_e = jnp.minimum(wide[rows - 1 : rows, :cols], wide[rows : rows + 1, :cols])
+    last_n = jnp.minimum(wide[:rows, cols - 1 : cols], wide[:rows, cols : cols + 1])
+    open_w = jnp.minimum(wide[0:1, :cols], wide[-1:, :cols])
+    open_s = jnp.minimum(wide[:rows, 0:1], wide[:rows, -1:])
 
     for copy in edges:
         copy.wait()
@@ -328,35 +336,46 @@
     from_south[...] = advect_scale * flux_s
     from_north[...] = advect_scale * flux_n
 
-    def add_rim(k, carry):
+    middle = [jnp.zeros((rows, cols - 2 * LANES), F32)] if cols > 2 * LANES else []
+
+    def forward(k, x):
         one = pl.ds(k, 1)
-        value[k, 0:1, :] += from_west[0, one, :]
-        value[k, rows - 1 : rows, :] -= from_west[1, one, :]
-        value[k, :, low] += jnp.where(lane == 0, pltpu.roll(from_south[...], LANES - k, 1), 0.0)
-        value[k, :, high] -= jnp.where(
-            lane == LANES - 1, pltpu.roll(from_north[...], LANES - 1 - k, 1), 0.0
+        rim = jnp.concatenate(
+            [
+                jnp.where(lane == 0, pltpu.roll(from_south[...], LANES - k, 1), 0.0),
+                *middle,
+                jnp.where(
+                    lane == LANES - 1, -pltpu.roll(from_north[...], LANES - 1 - k, 1), 0.0
+                ),
+            ],
+            axis=1,
         )
-        return carry
-
-    by_level(levels, add_rim, 0)
-
-    def forward(k, x):
-        x = (value[k] + mix[k] * x) * scale[k]
-        value[k] = x
+        source = value[k] + rim
+        source = jnp.concatenate(
+            [
+                source[:BAND] + jnp.where(band_row == 0, from_west[0, one, :], 0.0),
+                source[BAND : rows - BAND],
+                source[rows - BAND :]
+                - jnp.where(band_row == BAND - 1, from_west[1, one, :], 0.0),
+            ],
+            axis=0,
+        )
+        x = (source + coupling[k] * x) * scale[k]
+        temp[k] = x
         return x
 
-    x = by_level(levels, forward, jnp.zeros(tile, F32))
+    by_level(levels, forward, jnp.zeros(tile, F32))
 
     slope = force_scale / levels
 
     def backward(step, carry):
         x, tail = carry
         k = levels - 1 - step
-        x = value[k] + factor[k] * x
+        x = temp[k] + factor[k] * x
         temp_out[k] = x
-        part = slope * x
-        tail = tail + part
-        factor[k] = tail - 0.5 * part
+        share = slope * x
+        tail = tail + share
+        value[k] = tail - 0.5 * share
         return x, tail
 
     x, tail = by_level(levels, backward, (jnp.zeros(tile, F32), jnp.zeros(tile, F32)))
@@ -365,10 +384,10 @@
     def pack_press(k, carry):
         to_north, to_south = carry
         one = pl.ds(k, 1)
-        press_row[0, one, :] = factor[k, 0:1, :]
-        press_row[1, one, :] = factor[k, rows - 1 : rows, :]
-        to_north = fill(k, to_north, lane, factor[k, :, high], k + 1)
-        to_south = fill(k, to_south, lane, factor[k, :, low], k)
+        press_row[0, one, :] = value[k, 0:1, :]
+        press_row[1, one, :] = value[k, rows - 1 : rows, :]
+        to_north = fill(k, to_north, lane, value[k, :, high], k + 1)
+        to_south = fill(k, to_south, lane, value[k, :, low], k)
         return to_north, to_south
 
     to_north, to_south = by_level(levels, pack_press, (zero_side, zero_side))
@@ -385,12 +404,11 @@
 
     def momentum(k, carry):
         level = jnp.asarray(k, F32)
-        part = [pl.ds(at * BAND, BAND) for at in range(strips)]
-        here = factor[k, part[0], :] - tail_ref[part[0], :]
+        here = value[k, part[0], :] - tail_ref[part[0], :]
         turned = pltpu.roll(here, BAND - 1, 0)
         for at in range(strips):
             if at + 1 < strips:
-                later = factor[k, part[at + 1], :] - tail_ref[part[at + 1], :]
+                later = value[k, part[at + 1], :] - tail_ref[part[at + 1], :]
                 later_turned = pltpu.roll(later, BAND - 1, 0)
                 there = jnp.where(band_row == BAND - 1, later_turned, turned)
             else:
@@ -432,16 +450,19 @@
 
     by_level(levels, add_last, 0)
 
+    source = source_scale * joined(1, surf, bands, sides, corners)
+    root = jnp.sqrt(wide / levels)
+    inverse = 1.0 / (damping + root * around_total(root))
+    root_out[...] = root
+    ratio_out[...] = root * inverse
+
     for copy in total_copies:
         copy.wait()
     total_e = joined(0, totals, total_bands, total_sides, total_corners)
     total_n = joined(1, totals, total_bands, total_sides, total_corners)
     divergence = total_e - before(total_e, 0) + total_n - before(total_n, 1)
-    root = root_out[...]
-    inverse = 1.0 / (damping + root * around_total(root))
-    scaled_out[...] -= jnp.where(
-        root > 0.0, inverse * ((divergence_scale / levels) * divergence), 0.0
-    )
+    forcing = source - (divergence_scale / levels) * divergence
+    scaled_out[...] = jnp.where(root > 0.0, forcing * inverse, 0.0)
 
 
 def surface_kernel(
@@ -492,9 +513,7 @@
         out_shape=[field, pltpu.VMEM((2, levels, rows, cols), F32), wide, wide, wide],
         in_specs=[pl.BlockSpec(memory_space=pltpu.HBM)] * 6,
         out_specs=[vmem] * 5,
-        scratch_shapes=[field] * 3
-        + [pltpu.VMEM((levels + 1, rows, cols), F32)]
-        + [field] * 3
+        scratch_shapes=[field] * 8
         + [plane_int] * 2
         + [plane] * 3
         + [two_planes, two_planes, plane]
@@ -509,6 +528,10 @@
         ),
         name="columns",
     )(*inputs)
+    held = [
+        pltpu.with_memory_space_constraint(array, pltpu.VMEM)
+        for array in (temp_next, speed_next, root, ratio, scaled)
+    ]
     return pl.pallas_call(
         surface_kernel,
         out_shape=[
@@ -519,9 +542,9 @@
         in_specs=[vmem] * 5,
         out_specs=[pl.BlockSpec(memory_space=pltpu.HBM)] * 2 + [vmem],
         scratch_shapes=[pltpu.SemaphoreType.DMA((3,))],
-        compiler_params=pltpu.CompilerParams(vmem_limit_bytes=48 * 2**20),
+        compiler_params=pltpu.CompilerParams(vmem_limit_bytes=32 * 2**20),
         name="surface",
-    )(temp_next, speed_next, root, ratio, scaled)
+    )(*held)
 
 
 def solution(mesh):

time: 41.3 us -> 31.8 us (0.77)
  Pallas kernels: 38.2 us -> 31 us
  local copies, waits for them, and re-layouts: 2.29 us -> 0 us
    pallas_call x1, Pallas kernels: 31.8 us -> 27.1 us  [local(): pl.pallas_call(columns_kernel, out_shape=[field, pltpu.VMEM((2, levels, r...]
    pallas_call x1, Pallas kernels: 6.36 us -> 3.89 us  [local(): pl.pallas_call(surface_kernel, out_shape=[jax.ShapeDtypeStruct(temp.shape...]
    unnamed x2 -> x0, local copies, waits for them, and re-layouts: 2.29 us -> none
where the time goes in v3:
time: 31.8 us; the launch traced here: 31.6 us
  Pallas kernels  31 us (97%)
  between operations  0.64 us (2%)
    pallas_call x1, Pallas kernels, local(): pl.pallas_call(columns_kernel, out_shape=[field, pltpu.VMEM((2, levels, r...  27.1 us
    pallas_call x1, Pallas kernels, local(): pl.pallas_call(surface_kernel, out_shape=[jax.ShapeDtypeStruct(temp.shape...  3.89 us

profile of v3, /device:TPU:0, one launch (start us, length us, event | category | flops | bytes accessed | tf_op | source)
XLA Modules:
  0.0 31.6 jit_solution(1508325611706850670)
XLA Ops:
  0.6 27.1 %columns.1 = (f32[40,64,256]{2,1,0:T(8,128)S(1)}, f32[2,40,64,256]{3,2,1,0:T(8,128)S(1)}, f32[80,384]{1,0:T(8,128)S(1)}, f32[80,384]{1,0:T(8,128)S(1)}, f32[80,384]{1,0:T(8,128)S(1)}) custom-call(f32[40,64,256]{2,1,0:T(8,128)} %temp_hbm.1, f32[2,40,64,256]{3,2,1,0:T(8,128)} %speed_hbm.1, f32[40,64,256]{2,1,0:T(8,128)} %mix_hbm.1, s32[64,256]{1,0:T(8,128)} %sea_hbm.1, ...), custom_call_target="tpu_custom_call" | custom-call | tf_op jit(solution)/shard_map/columns/pallas_call | solution.py:511
  27.7 3.9 %surface.1 = (f32[40,64,256]{2,1,0:T(8,128)}, f32[2,40,64,256]{3,2,1,0:T(8,128)}, f32[64,256]{1,0:T(8,128)}) custom-call(f32[40,64,256]{2,1,0:T(8,128)S(1)} %get-tuple-element.8.temp_in, f32[2,40,64,256]{3,2,1,0:T(8,128)S(1)} %get-tuple-element.9.speed_in, f32[80,384]{1,0:T(8,128)S(1)} %get-tuple-element.10.root_in, ...), custom_call_target="tpu_custom_call" | custom-call | tf_op jit(solution)/shard_map/surface/pallas_call | solution.py:535

commit v4 on v3

--- a/solution.py
+++ b/solution.py
@@ -160,7 +160,6 @@
     value,
     factor,
     scale,
-    coupling,
     sea,
     tally,
     depth,
@@ -184,6 +183,7 @@
     fix_row,
     fix_col,
     load_sems,
+    chunk_sems,
     edge_sems,
     bands,
     sides,
@@ -197,21 +197,49 @@
     levels, rows, cols = temp.shape
     strips = rows // BAND
     greet_neighbours()
-    pairs = [
-        (sea_hbm, sea),
-        (tally_hbm, tally),
-        (rain_hbm, surf.at[1]),
-        (temp_hbm, temp),
-        (speed_hbm.at[0], east),
-        (speed_hbm.at[1], north),
-        (mix_hbm, mix),
-    ]
-    loads = [
-        pltpu.make_async_copy(src, dst, load_sems.at[at]) for at, (src, dst) in enumerate(pairs)
-    ]
-    for copy in loads:
+    low, high = slice(0, LANES), slice(cols - LANES, cols)
+    last_rows, last_lanes = pl.ds(rows - BAND, BAND), pl.ds(cols - LANES, LANES)
+    other_rows, other_lanes = pl.ds(0, rows - BAND), pl.ds(0, cols - LANES)
+    first_loads = [
+        pltpu.make_async_copy(src, dst, load_sems.at[at])
+        for at, (src, dst) in enumerate(
+            (
+                (sea_hbm, sea),
+                (tally_hbm, tally),
+                (rain_hbm, surf.at[1]),
+                (temp_hbm, temp),
+                (speed_hbm.at[1, :, :, last_lanes], north.at[:, :, last_lanes]),
+                (speed_hbm.at[0, :, last_rows, :], east.at[:, last_rows, :]),
+            )
+        )
+    ]
+    for copy in first_loads:
         copy.start()
-    for copy in loads[:3]:
+    chunks = levels // GROUP
+
+    def load_mix(at):
+        span = pl.ds(at * GROUP, GROUP)
+        return pltpu.make_async_copy(mix_hbm.at[span], mix.at[span], chunk_sems.at[0, at])
+
+    def load_speeds(at):
+        span = pl.ds(at * GROUP, GROUP)
+        return [
+            pltpu.make_async_copy(
+                speed_hbm.at[0, span, other_rows, :],
+                east.at[span, other_rows, :],
+                chunk_sems.at[1, at],
+            ),
+            pltpu.make_async_copy(
+                speed_hbm.at[1, span, :, other_lanes],
+                north.at[span, :, other_lanes],
+                chunk_sems.at[2, at],
+            ),
+        ]
+
+    for at in range(chunks):
+        for copy in (load_mix(at), *load_speeds(at)):
+            copy.start()
+    for copy in first_loads[:3]:
         copy.wait()
 
     tile = (rows, cols)
@@ -229,7 +257,6 @@
 
     lane = lane_index((rows, LANES))
     zero_side = jnp.zeros((rows, LANES), F32)
-    low, high = slice(0, LANES), slice(cols - LANES, cols)
     def pack_temp(k, carry):
         to_north, to_south = carry
         one = pl.ds(k, 1)
@@ -243,7 +270,7 @@
         row_east[1, pl.ds(k, 1), :] = east[k, rows - 1 : rows, :]
         return fill(k + HALF, to_north, lane, north[k, :, high], k + 1 + HALF)
 
-    loads[3].wait()
+    first_loads[3].wait()
     to_north, to_south = by_level(levels, pack_temp, (zero_side, zero_side))
     col_south[...] = to_south
     meet_neighbours()
@@ -252,15 +279,13 @@
         send(row_west, from_east, edge_sems, 0, -1, 0),
         send(col_south, from_north, edge_sems, 1, 0, -1),
     ]
-    loads[4].wait()
-    loads[5].wait()
+    first_loads[4].wait()
+    first_loads[5].wait()
     col_north[...] = by_level(levels, pack_speed, to_north)
     edges += [
         send(row_east, from_west, edge_sems, 2, 1, 0),
         send(col_north, from_south, edge_sems, 3, 0, 1),
     ]
-
-    loads[6].wait()
 
     band = (BAND, cols)
     band_row = row_index(band)
@@ -279,7 +304,8 @@
         here = temp[k, part[0], :]
         turned = pltpu.roll(here, BAND - 1, 0)
         for at in range(strips):
-            above, keep = carry[at]
+            keep = carry[at]
+            above = jnp.where(level < depth[part[at], :], mix[k, part[at], :], 0.0)
             if at + 1 < strips:
                 later = temp[k, part[at + 1], :]
                 later_turned = pltpu.roll(later, BAND - 1, 0)
@@ -295,7 +321,6 @@
             )
             total = total + (flux - before(flux, 1))
             value[k, part[at], :] = here - advect_scale * total
-            coupling[k, part[at], :] = above
             below = jnp.where(
                 level + 1.0 < depth[part[at], :], mix[later_level, part[at], :], 0.0
             )
@@ -303,13 +328,27 @@
             scale[k, part[at], :] = inverse_pivot
             leading = below * inverse_pivot
             factor[k, part[at], :] = leading
-            result.append((below, 1.0 - leading))
+            result.append(1.0 - leading)
             if at + 1 < strips:
                 here, turned = later, later_turned
         return tuple(result)
 
-    nothing = jnp.zeros(band, F32)
-    lax.fori_loop(0, levels, assemble, ((nothing, nothing),) * strips)
+    def assemble_chunk(at, carry):
+        @pl.when(at + 1 < chunks)
+        def _():
+            load_mix(at + 1).wait()
+
+        for copy in load_speeds(at):
+            copy.wait()
+
+        def step(half, carry):
+            k = at * GROUP + 2 * half
+            return assemble(k + 1, assemble(k, carry))
+
+        return lax.fori_loop(0, GROUP // 2, step, carry)
+
+    load_mix(0).wait()
+    lax.fori_loop(0, chunks, assemble_chunk, (jnp.zeros(band, F32),) * strips)
 
     for copy in surf_copies:
         copy.wait()
@@ -360,7 +399,8 @@
             ],
             axis=0,
         )
-        x = (source + coupling[k] * x) * scale[k]
+        above = jnp.where(jnp.asarray(k, F32) < depth[...], mix[k], 0.0)
+        x = (source + above * x) * scale[k]
         temp[k] = x
         return x
 
@@ -369,28 +409,26 @@
     slope = force_scale / levels
 
     def backward(step, carry):
-        x, tail = carry
+        x, tail, to_north, to_south = carry
         k = levels - 1 - step
+        one = pl.ds(k, 1)
         x = temp[k] + factor[k] * x
         temp_out[k] = x
         share = slope * x
         tail = tail + share
-        value[k] = tail - 0.5 * share
-        return x, tail
-
-    x, tail = by_level(levels, backward, (jnp.zeros(tile, F32), jnp.zeros(tile, F32)))
+        press = tail - 0.5 * share
+        value[k] = press
+        press_row[0, one, :] = press[0:1, :]
+        press_row[1, one, :] = press[rows - 1 : rows, :]
+        to_north = fill(k, to_north, lane, press[:, high], k + 1)
+        to_south = fill(k, to_south, lane, press[:, low], k)
+        return x, tail, to_north, to_south
+
+    zero_tile = jnp.zeros(tile, F32)
+    x, tail, to_north, to_south = by_level(
+        levels, backward, (zero_tile, zero_tile, zero_side, zero_side)
+    )
     tail_ref[...] = tail
-
-    def pack_press(k, carry):
-        to_north, to_south = carry
-        one = pl.ds(k, 1)
-        press_row[0, one, :] = value[k, 0:1, :]
-        press_row[1, one, :] = value[k, rows - 1 : rows, :]
-        to_north = fill(k, to_north, lane, value[k, :, high], k + 1)
-        to_south = fill(k, to_south, lane, value[k, :, low], k)
-        return to_north, to_south
-
-    to_north, to_south = by_level(levels, pack_press, (zero_side, zero_side))
     press_row[0] -= tail[0:1, :]
     press_row[1] -= tail[rows - 1 : rows, :]
     press_col[0] = to_south - tail[:, 0:1]
@@ -513,7 +551,7 @@
         out_shape=[field, pltpu.VMEM((2, levels, rows, cols), F32), wide, wide, wide],
         in_specs=[pl.BlockSpec(memory_space=pltpu.HBM)] * 6,
         out_specs=[vmem] * 5,
-        scratch_shapes=[field] * 8
+        scratch_shapes=[field] * 7
         + [plane_int] * 2
         + [plane] * 3
         + [two_planes, two_planes, plane]
@@ -521,7 +559,11 @@
         + [col_set] * 4
         + [row_sets, row_set, col_sets, col_set]
         + [row_set, col_set]
-        + [pltpu.SemaphoreType.DMA((7,)), pltpu.SemaphoreType.DMA((2, 6))]
+        + [
+            pltpu.SemaphoreType.DMA((6,)),
+            pltpu.SemaphoreType.DMA((3, levels // GROUP)),
+            pltpu.SemaphoreType.DMA((2, 6)),
+        ]
         + halo_shapes(rows, cols) * 2,
         compiler_params=pltpu.CompilerParams(
             collective_id=0, has_side_effects=True, vmem_limit_bytes=48 * 2**20

time: 31.8 us -> 29.3 us (0.921)
  Pallas kernels: 31 us -> 28.5 us
    pallas_call x1, Pallas kernels: 27.1 us -> 24.6 us  [local(): pl.pallas_call(columns_kernel, out_shape=[field, pltpu.VMEM((2, levels, r...]
where the time goes in v4:
time: 29.3 us; the launch traced here: 29.2 us
  Pallas kernels  28.5 us (97%)
  between operations  0.64 us (2%)
    pallas_call x1, Pallas kernels, local(): pl.pallas_call(columns_kernel, out_shape=[field, pltpu.VMEM((2, levels, r...  24.6 us
    pallas_call x1, Pallas kernels, local(): pl.pallas_call(surface_kernel, out_shape=[jax.ShapeDtypeStruct(temp.shape...  3.89 us

profile of v4, /device:TPU:0, one launch (start us, length us, event | category | flops | bytes accessed | tf_op | source)
XLA Modules:
  0.0 29.2 jit_solution(4284941639428450702)
XLA Ops:
  0.6 24.6 %columns.1 = (f32[40,64,256]{2,1,0:T(8,128)S(1)}, f32[2,40,64,256]{3,2,1,0:T(8,128)S(1)}, f32[80,384]{1,0:T(8,128)S(1)}, f32[80,384]{1,0:T(8,128)S(1)}, f32[80,384]{1,0:T(8,128)S(1)}) custom-call(f32[40,64,256]{2,1,0:T(8,128)} %temp_hbm.1, f32[2,40,64,256]{3,2,1,0:T(8,128)} %speed_hbm.1, f32[40,64,256]{2,1,0:T(8,128)} %mix_hbm.1, s32[64,256]{1,0:T(8,128)} %sea_hbm.1, ...), custom_call_target="tpu_custom_call" | custom-call | tf_op jit(solution)/shard_map/columns/pallas_call | solution.py:549
  25.3 3.9 %surface.1 = (f32[40,64,256]{2,1,0:T(8,128)}, f32[2,40,64,256]{3,2,1,0:T(8,128)}, f32[64,256]{1,0:T(8,128)}) custom-call(f32[40,64,256]{2,1,0:T(8,128)S(1)} %get-tuple-element.8.temp_in, f32[2,40,64,256]{3,2,1,0:T(8,128)S(1)} %get-tuple-element.9.speed_in, f32[80,384]{1,0:T(8,128)S(1)} %get-tuple-element.10.root_in, ...), custom_call_target="tpu_custom_call" | custom-call | tf_op jit(solution)/shard_map/surface/pallas_call | solution.py:577

commit v5 on v4

--- a/solution.py
+++ b/solution.py
@@ -198,19 +198,10 @@
     strips = rows // BAND
     greet_neighbours()
     low, high = slice(0, LANES), slice(cols - LANES, cols)
-    last_rows, last_lanes = pl.ds(rows - BAND, BAND), pl.ds(cols - LANES, LANES)
-    other_rows, other_lanes = pl.ds(0, rows - BAND), pl.ds(0, cols - LANES)
     first_loads = [
         pltpu.make_async_copy(src, dst, load_sems.at[at])
         for at, (src, dst) in enumerate(
-            (
-                (sea_hbm, sea),
-                (tally_hbm, tally),
-                (rain_hbm, surf.at[1]),
-                (temp_hbm, temp),
-                (speed_hbm.at[1, :, :, last_lanes], north.at[:, :, last_lanes]),
-                (speed_hbm.at[0, :, last_rows, :], east.at[:, last_rows, :]),
-            )
+            ((sea_hbm, sea), (tally_hbm, tally), (rain_hbm, surf.at[1]))
         )
     ]
     for copy in first_loads:
@@ -221,25 +212,21 @@
         span = pl.ds(at * GROUP, GROUP)
         return pltpu.make_async_copy(mix_hbm.at[span], mix.at[span], chunk_sems.at[0, at])
 
-    def load_speeds(at):
+    def load_rest(at):
         span = pl.ds(at * GROUP, GROUP)
         return [
-            pltpu.make_async_copy(
-                speed_hbm.at[0, span, other_rows, :],
-                east.at[span, other_rows, :],
-                chunk_sems.at[1, at],
-            ),
-            pltpu.make_async_copy(
-                speed_hbm.at[1, span, :, other_lanes],
-                north.at[span, :, other_lanes],
-                chunk_sems.at[2, at],
-            ),
+            pltpu.make_async_copy(temp_hbm.at[span], temp.at[span], chunk_sems.at[1, at]),
+            pltpu.make_async_copy(speed_hbm.at[0, span], east.at[span], chunk_sems.at[2, at]),
+            pltpu.make_async_copy(speed_hbm.at[1, span], north.at[span], chunk_sems.at[3, at]),
         ]
 
+    load_mix(0).start()
     for at in range(chunks):
-        for copy in (load_mix(at), *load_speeds(at)):
+        for copy in load_rest(at):
             copy.start()
-    for copy in first_loads[:3]:
+        if at + 1 < chunks:
+            load_mix(at + 1).start()
+    for copy in first_loads:
         copy.wait()
 
     tile = (rows, cols)
@@ -257,36 +244,6 @@
 
     lane = lane_index((rows, LANES))
     zero_side = jnp.zeros((rows, LANES), F32)
-    def pack_temp(k, carry):
-        to_north, to_south = carry
-        one = pl.ds(k, 1)
-        row_east[0, one, :] = temp[k, rows - 1 : rows, :]
-        row_west[one, :] = temp[k, 0:1, :]
-        to_north = fill(k, to_north, lane, temp[k, :, high], k + 1)
-        to_south = fill(k, to_south, lane, temp[k, :, low], k)
-        return to_north, to_south
-
-    def pack_speed(k, to_north):
-        row_east[1, pl.ds(k, 1), :] = east[k, rows - 1 : rows, :]
-        return fill(k + HALF, to_north, lane, north[k, :, high], k + 1 + HALF)
-
-    first_loads[3].wait()
-    to_north, to_south = by_level(levels, pack_temp, (zero_side, zero_side))
-    col_south[...] = to_south
-    meet_neighbours()
-    surf_copies = start_halo(surf, bands, sides, corners, halo_sems)
-    edges = [
-        send(row_west, from_east, edge_sems, 0, -1, 0),
-        send(col_south, from_north, edge_sems, 1, 0, -1),
-    ]
-    first_loads[4].wait()
-    first_loads[5].wait()
-    col_north[...] = by_level(levels, pack_speed, to_north)
-    edges += [
-        send(row_east, from_west, edge_sems, 2, 1, 0),
-        send(col_north, from_south, edge_sems, 3, 0, 1),
-    ]
-
     band = (BAND, cols)
     band_row = row_index(band)
 
@@ -338,17 +295,52 @@
         def _():
             load_mix(at + 1).wait()
 
-        for copy in load_speeds(at):
-            copy.wait()
-
         def step(half, carry):
             k = at * GROUP + 2 * half
             return assemble(k + 1, assemble(k, carry))
 
         return lax.fori_loop(0, GROUP // 2, step, carry)
 
+    def assemble_early(at, carry):
+        for copy in load_rest(at):
+            copy.wait()
+        return assemble_chunk(at, carry)
+
+    early = min(2, chunks)
     load_mix(0).wait()
-    lax.fori_loop(0, chunks, assemble_chunk, (jnp.zeros(band, F32),) * strips)
+    carry = lax.fori_loop(0, early, assemble_early, (jnp.zeros(band, F32),) * strips)
+    for at in range(early, chunks):
+        for copy in load_rest(at):
+            copy.wait()
+
+    def pack_temp(k, carry):
+        to_north, to_south = carry
+        one = pl.ds(k, 1)
+        row_east[0, one, :] = temp[k, rows - 1 : rows, :]
+        row_west[one, :] = temp[k, 0:1, :]
+        to_north = fill(k, to_north, lane, temp[k, :, high], k + 1)
+        to_south = fill(k, to_south, lane, temp[k, :, low], k)
+        return to_north, to_south
+
+    def pack_speed(k, to_north):
+        row_east[1, pl.ds(k, 1), :] = east[k, rows - 1 : rows, :]
+        return fill(k + HALF, to_north, lane, north[k, :, high], k + 1 + HALF)
+
+    to_north, to_south = by_level(levels, pack_temp, (zero_side, zero_side))
+    col_south[...] = to_south
+    meet_neighbours()
+    surf_copies = start_halo(surf, bands, sides, corners, halo_sems)
+    edges = [
+        send(row_west, from_east, edge_sems, 0, -1, 0),
+        send(col_south, from_north, edge_sems, 1, 0, -1),
+    ]
+    col_north[...] = by_level(levels, pack_speed, to_north)
+    edges += [
+        send(row_east, from_west, edge_sems, 2, 1, 0),
+        send(col_north, from_south, edge_sems, 3, 0, 1),
+    ]
+
+    lax.fori_loop(early, chunks, assemble_chunk, carry)
 
     for copy in surf_copies:
         copy.wait()
@@ -507,10 +499,14 @@
     temp_in, speed_in, root_in, ratio_in, scaled_in, temp_out, speed_out, out, sems
 ):
     rows, cols = out.shape
+    pairs = [(temp_in, temp_out)] + [(speed_in.at[at], speed_out.at[at]) for at in range(2)]
+    chunk = temp_in.shape[0] // sems.shape[1]
     copies = [
-        pltpu.make_async_copy(temp_in, temp_out, sems.at[0]),
-        pltpu.make_async_copy(speed_in.at[0], speed_out.at[0], sems.at[1]),
-        pltpu.make_async_copy(speed_in.at[1], speed_out.at[1], sems.at[2]),
+        pltpu.make_async_copy(
+            src.at[pl.ds(at * chunk, chunk)], dst.at[pl.ds(at * chunk, chunk)], sems.at[which, at]
+        )
+        for at in range(sems.shape[1])
+        for which, (src, dst) in enumerate(pairs)
     ]
     for copy in copies:
         copy.start()
@@ -560,8 +556,8 @@
         + [row_sets, row_set, col_sets, col_set]
         + [row_set, col_set]
         + [
-            pltpu.SemaphoreType.DMA((6,)),
-            pltpu.SemaphoreType.DMA((3, levels // GROUP)),
+            pltpu.SemaphoreType.DMA((3,)),
+            pltpu.SemaphoreType.DMA((4, levels // GROUP)),
             pltpu.SemaphoreType.DMA((2, 6)),
         ]
         + halo_shapes(rows, cols) * 2,
@@ -583,7 +579,7 @@
         ],
         in_specs=[vmem] * 5,
         out_specs=[pl.BlockSpec(memory_space=pltpu.HBM)] * 2 + [vmem],
-        scratch_shapes=[pltpu.SemaphoreType.DMA((3,))],
+        scratch_shapes=[pltpu.SemaphoreType.DMA((3, levels // GROUP))],
         compiler_params=pltpu.CompilerParams(vmem_limit_bytes=32 * 2**20),
         name="surface",
     )(*held)

time: 29.3 us -> 32.9 us (1.12)
  Pallas kernels: 28.5 us -> 31.9 us
    pallas_call x1, Pallas kernels: 24.6 us -> 28 us  [local(): pl.pallas_call(columns_kernel, out_shape=[field, pltpu.VMEM((2, levels, r...]
where the time goes in v5:
time: 32.9 us; the launch traced here: 32.5 us
  Pallas kernels  31.9 us (97%)
  between operations  0.64 us (2%)
    pallas_call x1, Pallas kernels, local(): pl.pallas_call(columns_kernel, out_shape=[field, pltpu.VMEM((2, levels, r...  28 us
    pallas_call x1, Pallas kernels, local(): pl.pallas_call(surface_kernel, out_shape=[jax.ShapeDtypeStruct(temp.shape...  3.89 us

profile of v5, /device:TPU:0, one launch (start us, length us, event | category | flops | bytes accessed | tf_op | source)
XLA Modules:
  0.0 32.5 jit_solution(8982850799501959354)
XLA Ops:
  0.6 28.0 %columns.1 = (f32[40,64,256]{2,1,0:T(8,128)S(1)}, f32[2,40,64,256]{3,2,1,0:T(8,128)S(1)}, f32[80,384]{1,0:T(8,128)S(1)}, f32[80,384]{1,0:T(8,128)S(1)}, f32[80,384]{1,0:T(8,128)S(1)}) custom-call(f32[40,64,256]{2,1,0:T(8,128)} %temp_hbm.1, f32[2,40,64,256]{3,2,1,0:T(8,128)} %speed_hbm.1, f32[40,64,256]{2,1,0:T(8,128)} %mix_hbm.1, s32[64,256]{1,0:T(8,128)} %sea_hbm.1, ...), custom_call_target="tpu_custom_call" | custom-call | tf_op jit(solution)/shard_map/columns/pallas_call | solution.py:545
  28.7 3.9 %surface.1 = (f32[40,64,256]{2,1,0:T(8,128)}, f32[2,40,64,256]{3,2,1,0:T(8,128)}, f32[64,256]{1,0:T(8,128)}) custom-call(f32[40,64,256]{2,1,0:T(8,128)S(1)} %get-tuple-element.8.temp_in, f32[2,40,64,256]{3,2,1,0:T(8,128)S(1)} %get-tuple-element.9.speed_in, f32[80,384]{1,0:T(8,128)S(1)} %get-tuple-element.10.root_in, ...), custom_call_target="tpu_custom_call" | custom-call | tf_op jit(solution)/shard_map/surface/pallas_call | solution.py:573

commit v6 on v4

--- a/solution.py
+++ b/solution.py
@@ -20,6 +20,7 @@
 LANES = 128
 HALF = LANES // 2
 GROUP = 8
+QUAD = 4
 BAND = 8
 F32 = jnp.float32
 AROUND = ((1, 0), (-1, 0), (0, 1), (0, -1), (1, 1), (1, -1), (-1, 1), (-1, -1))
@@ -296,41 +297,48 @@
 
     part = [pl.ds(at * BAND, BAND) for at in range(strips)]
 
-    def assemble(k, carry):
-        level = jnp.asarray(k, F32)
-        later_level = jnp.minimum(k + 1, levels - 1)
+    def neighbour_rows(read, at, here, turned):
+        if at + 1 == strips:
+            return turned, None, None
+        later = read(at + 1)
+        later_turned = pltpu.roll(later, BAND - 1, 0)
+        return jnp.where(band_row == BAND - 1, later_turned, turned), later, later_turned
+
+    def assemble(first, carry):
+        ks = [first + at for at in range(QUAD)]
+        reads = [lambda at, k=k: temp[k, part[at], :] for k in ks]
+        heres = [read(0) for read in reads]
+        turns = [pltpu.roll(here, BAND - 1, 0) for here in heres]
+        previous = [jnp.zeros(band, F32)] * QUAD
         result = []
-        previous = jnp.zeros(band, F32)
-        here = temp[k, part[0], :]
-        turned = pltpu.roll(here, BAND - 1, 0)
         for at in range(strips):
             keep = carry[at]
-            above = jnp.where(level < depth[part[at], :], mix[k, part[at], :], 0.0)
-            if at + 1 < strips:
-                later = temp[k, part[at + 1], :]
-                later_turned = pltpu.roll(later, BAND - 1, 0)
-                there = jnp.where(band_row == BAND - 1, later_turned, turned)
-            else:
-                there = turned
-            flux = upwind(depth_e[part[at], :], level, east[k, part[at], :], here, there)
-            turned_flux = pltpu.roll(flux, 1, 0)
-            total = flux - jnp.where(band_row == 0, previous, turned_flux)
-            previous = turned_flux
-            flux = upwind(
-                depth_n[part[at], :], level, north[k, part[at], :], here, after(here, 1)
-            )
-            total = total + (flux - before(flux, 1))
-            value[k, part[at], :] = here - advect_scale * total
-            below = jnp.where(
-                level + 1.0 < depth[part[at], :], mix[later_level, part[at], :], 0.0
-            )
-            inverse_pivot = inverse_of((1.0 + below) + above * keep)
-            scale[k, part[at], :] = inverse_pivot
-            leading = below * inverse_pivot
-            factor[k, part[at], :] = leading
-            result.append(1.0 - leading)
-            if at + 1 < strips:
-                here, turned = later, later_turned
+            wet = depth[part[at], :]
+            wet_e = depth_e[part[at], :]
+            wet_n = depth_n[part[at], :]
+            above = jnp.where(jnp.asarray(first, F32) < wet, mix[first, part[at], :], 0.0)
+            for q, k in enumerate(ks):
+                level = jnp.asarray(k, F32)
+                here = heres[q]
+                there, heres[q], next_turn = neighbour_rows(reads[q], at, here, turns[q])
+                turns[q] = next_turn
+                flux = upwind(wet_e, level, east[k, part[at], :], here, there)
+                turned_flux = pltpu.roll(flux, 1, 0)
+                total = flux - jnp.where(band_row == 0, previous[q], turned_flux)
+                previous[q] = turned_flux
+                flux = upwind(wet_n, level, north[k, part[at], :], here, after(here, 1))
+                total = total + (flux - before(flux, 1))
+                value[k, part[at], :] = here - advect_scale * total
+                below = jnp.where(
+                    level + 1.0 < wet, mix[jnp.minimum(k + 1, levels - 1), part[at], :], 0.0
+                )
+                inverse_pivot = inverse_of((1.0 + below) + above * keep)
+                scale[k, part[at], :] = inverse_pivot
+                leading = below * inverse_pivot
+                factor[k, part[at], :] = leading
+                keep = 1.0 - leading
+                above = below
+            result.append(keep)
         return tuple(result)
 
     def assemble_chunk(at, carry):
@@ -342,10 +350,9 @@
             copy.wait()
 
         def step(half, carry):
-            k = at * GROUP + 2 * half
-            return assemble(k + 1, assemble(k, carry))
-
-        return lax.fori_loop(0, GROUP // 2, step, carry)
+            return assemble(at * GROUP + QUAD * half, carry)
+
+        return lax.fori_loop(0, GROUP // QUAD, step, carry)
 
     load_mix(0).wait()
     lax.fori_loop(0, chunks, assemble_chunk, (jnp.zeros(band, F32),) * strips)
@@ -440,30 +447,33 @@
 
     totals[...] = jnp.zeros(totals.shape, F32)
 
-    def momentum(k, carry):
-        level = jnp.asarray(k, F32)
-        here = value[k, part[0], :] - tail_ref[part[0], :]
-        turned = pltpu.roll(here, BAND - 1, 0)
+    def momentum(step, carry):
+        ks = [step * QUAD + at for at in range(QUAD)]
+        reads = [lambda at, k=k: value[k, part[at], :] - tail_ref[part[at], :] for k in ks]
+        heres = [read(0) for read in reads]
+        turns = [pltpu.roll(here, BAND - 1, 0) for here in heres]
         for at in range(strips):
-            if at + 1 < strips:
-                later = value[k, part[at + 1], :] - tail_ref[part[at + 1], :]
-                later_turned = pltpu.roll(later, BAND - 1, 0)
-                there = jnp.where(band_row == BAND - 1, later_turned, turned)
-            else:
-                there = turned
-            speed = east[k, part[at], :] + (here - there)
-            speed = jnp.where(level < depth_e[part[at], :], speed, 0.0)
-            speed_out[0, k, part[at], :] = speed
-            totals[0, part[at], :] += speed
-            speed = north[k, part[at], :] + (here - after(here, 1))
-            speed = jnp.where(level < depth_n[part[at], :], speed, 0.0)
-            speed_out[1, k, part[at], :] = speed
-            totals[1, part[at], :] += speed
-            if at + 1 < strips:
-                here, turned = later, later_turned
+            wet_e = depth_e[part[at], :]
+            wet_n = depth_n[part[at], :]
+            sums = [totals[0, part[at], :], totals[1, part[at], :]]
+            for q, k in enumerate(ks):
+                level = jnp.asarray(k, F32)
+                here = heres[q]
+                there, heres[q], next_turn = neighbour_rows(reads[q], at, here, turns[q])
+                turns[q] = next_turn
+                speed = east[k, part[at], :] + (here - there)
+                speed = jnp.where(level < wet_e, speed, 0.0)
+                speed_out[0, k, part[at], :] = speed
+                sums[0] = sums[0] + speed
+                speed = north[k, part[at], :] + (here - after(here, 1))
+                speed = jnp.where(level < wet_n, speed, 0.0)
+                speed_out[1, k, part[at], :] = speed
+                sums[1] = sums[1] + speed
+            totals[0, part[at], :] = sums[0]
+            totals[1, part[at], :] = sums[1]
         return carry
 
-    lax.fori_loop(0, levels, momentum, 0)
+    lax.fori_loop(0, levels // QUAD, momentum, 0)
 
     for copy in press:
         copy.wait()

time: 29.3 us -> 29.3 us (level)
  no operation moved by 1% of the time
where the time goes in v6:
time: 29.3 us; the launch traced here: 28.9 us
  Pallas kernels  28.3 us (97%)
  between operations  0.64 us (2%)
    pallas_call x1, Pallas kernels, local(): pl.pallas_call(columns_kernel, out_shape=[field, pltpu.VMEM((2, levels, r...  24.4 us
    pallas_call x1, Pallas kernels, local(): pl.pallas_call(surface_kernel, out_shape=[jax.ShapeDtypeStruct(temp.shape...  3.89 us

profile of v6, /device:TPU:0, one launch (start us, length us, event | category | flops | bytes accessed | tf_op | source)
XLA Modules:
  0.0 28.9 jit_solution(8825264371911310045)
XLA Ops:
  0.6 24.4 %columns.1 = (f32[40,64,256]{2,1,0:T(8,128)S(1)}, f32[2,40,64,256]{3,2,1,0:T(8,128)S(1)}, f32[80,384]{1,0:T(8,128)S(1)}, f32[80,384]{1,0:T(8,128)S(1)}, f32[80,384]{1,0:T(8,128)S(1)}) custom-call(f32[40,64,256]{2,1,0:T(8,128)} %temp_hbm.1, f32[2,40,64,256]{3,2,1,0:T(8,128)} %speed_hbm.1, f32[40,64,256]{2,1,0:T(8,128)} %mix_hbm.1, s32[64,256]{1,0:T(8,128)} %sea_hbm.1, ...), custom_call_target="tpu_custom_call" | custom-call | tf_op jit(solution)/shard_map/columns/pallas_call | solution.py:559
  25.0 3.9 %surface.1 = (f32[40,64,256]{2,1,0:T(8,128)}, f32[2,40,64,256]{3,2,1,0:T(8,128)}, f32[64,256]{1,0:T(8,128)}) custom-call(f32[40,64,256]{2,1,0:T(8,128)S(1)} %get-tuple-element.8.temp_in, f32[2,40,64,256]{3,2,1,0:T(8,128)S(1)} %get-tuple-element.9.speed_in, f32[80,384]{1,0:T(8,128)S(1)} %get-tuple-element.10.root_in, ...), custom_call_target="tpu_custom_call" | custom-call | tf_op jit(solution)/shard_map/surface/pallas_call | solution.py:587

commit v7 on v6

--- a/solution.py
+++ b/solution.py
@@ -181,6 +181,9 @@
     press_from_east,
     press_col,
     press_from_north,
+    last_row_low,
+    last_row_rest,
+    last_col,
     fix_row,
     fix_col,
     load_sems,
@@ -382,68 +385,96 @@
     from_south[...] = advect_scale * flux_s
     from_north[...] = advect_scale * flux_n
 
-    middle = [jnp.zeros((rows, cols - 2 * LANES), F32)] if cols > 2 * LANES else []
-
-    def forward(k, x):
+    rest = cols - LANES
+    whole_low = (rows, 0, LANES)
+    band_rest = (BAND, LANES, cols)
+    whole_rest = (rows, LANES, cols)
+
+    def forward(k, x, region):
+        size, start, stop = region
         one = pl.ds(k, 1)
-        rim = jnp.concatenate(
-            [
-                jnp.where(lane == 0, pltpu.roll(from_south[...], LANES - k, 1), 0.0),
-                *middle,
-                jnp.where(
-                    lane == LANES - 1, -pltpu.roll(from_north[...], LANES - 1 - k, 1), 0.0
-                ),
-            ],
-            axis=1,
-        )
-        source = value[k] + rim
-        source = jnp.concatenate(
-            [
-                source[:BAND] + jnp.where(band_row == 0, from_west[0, one, :], 0.0),
+        source = value[k, :size, start:stop]
+        if start == 0:
+            rim = jnp.where(lane == 0, pltpu.roll(from_south[...], LANES - k, 1), 0.0)
+        else:
+            turned = pltpu.roll(from_north[:size, :], LANES - 1 - k, 1)
+            rim = jnp.where(lane[:size] == LANES - 1, -turned, 0.0)
+            if rest > LANES:
+                rim = jnp.concatenate([jnp.zeros((size, rest - LANES), F32), rim], axis=1)
+        source = source + rim
+        row = band_row[:, : stop - start]
+        pieces = [source[:BAND] + jnp.where(row == 0, from_west[0, one, :][:, start:stop], 0.0)]
+        if size == rows:
+            pieces += [
                 source[BAND : rows - BAND],
                 source[rows - BAND :]
-                - jnp.where(band_row == BAND - 1, from_west[1, one, :], 0.0),
-            ],
-            axis=0,
+                - jnp.where(row == BAND - 1, from_west[1, one, :][:, start:stop], 0.0),
+            ]
+        source = jnp.concatenate(pieces, axis=0) if len(pieces) > 1 else pieces[0]
+        above = jnp.where(
+            jnp.asarray(k, F32) < depth[:size, start:stop], mix[k, :size, start:stop], 0.0
         )
-        above = jnp.where(jnp.asarray(k, F32) < depth[...], mix[k], 0.0)
-        x = (source + above * x) * scale[k]
-        temp[k] = x
+        x = (source + above * x) * scale[k, :size, start:stop]
+        temp[k, :size, start:stop] = x
         return x
 
-    by_level(levels, forward, jnp.zeros(tile, F32))
-
     slope = force_scale / levels
 
-    def backward(step, carry):
-        x, tail, to_north, to_south = carry
-        k = levels - 1 - step
-        one = pl.ds(k, 1)
-        x = temp[k] + factor[k] * x
-        temp_out[k] = x
+    def backward(k, x, tail, region):
+        size, start, stop = region
+        x = temp[k, :size, start:stop] + factor[k, :size, start:stop] * x
         share = slope * x
         tail = tail + share
         press = tail - 0.5 * share
-        value[k] = press
-        press_row[0, one, :] = press[0:1, :]
-        press_row[1, one, :] = press[rows - 1 : rows, :]
-        to_north = fill(k, to_north, lane, press[:, high], k + 1)
-        to_south = fill(k, to_south, lane, press[:, low], k)
-        return x, tail, to_north, to_south
-
-    zero_tile = jnp.zeros(tile, F32)
-    x, tail, to_north, to_south = by_level(
-        levels, backward, (zero_tile, zero_tile, zero_side, zero_side)
-    )
-    tail_ref[...] = tail
-    press_row[0] -= tail[0:1, :]
-    press_row[1] -= tail[rows - 1 : rows, :]
-    press_col[0] = to_south - tail[:, 0:1]
-    press_col[1] = to_north - tail[:, cols - 1 : cols]
+        if size == rows:
+            temp_out[k, :, start:stop] = x
+            value[k, :, start:stop] = press
+            last = last_row_low if start == 0 else last_row_rest
+            last[pl.ds(k, 1), :] = press[rows - 1 :, :]
+        return x, tail, press
+
+    zero_low = jnp.zeros((rows, LANES), F32)
+    zero_band = jnp.zeros((BAND, rest), F32)
+    zero_rest = jnp.zeros((rows, rest), F32)
+
+    def forward_first(k, carry):
+        return forward(k, carry[0], whole_low), forward(k, carry[1], band_rest)
+
+    def backward_first(step, carry):
+        x, tail, x_band, tail_band, packed = carry
+        k = levels - 1 - step
+        one = pl.ds(k, 1)
+        x, tail, press = backward(k, x, tail, whole_low)
+        packed = fill(k, packed, lane, press, k)
+        x_band, tail_band, press_band = backward(k, x_band, tail_band, band_rest)
+        press_row[one, :] = jnp.concatenate([press[0:1, :], press_band[0:1, :]], axis=1)
+        return x, tail, x_band, tail_band, packed
+
+    def backward_rest(step, carry):
+        x, tail, packed = carry
+        k = levels - 1 - step
+        x, tail, press = backward(k, x, tail, whole_rest)
+        packed = fill(k, packed, lane, press[:, rest - LANES :], k + 1)
+        return x, tail, packed
+
+    by_level(levels, forward_first, (zero_low, zero_band))
+    x, tail, x_band, tail_band, packed = by_level(
+        levels, backward_first, (zero_low, zero_low, zero_band, zero_band, zero_side)
+    )
+    tail_ref[:, :LANES] = tail
+    press_row[:, :LANES] -= tail[0:1, :]
+    press_row[:, LANES:] -= tail_band[0:1, :]
+    last_row_low[...] -= tail[rows - 1 :, :]
+    press_col[...] = packed - tail[:, 0:1]
     press = [
-        send(press_row.at[0], press_from_east, edge_sems, 4, -1, 0),
-        send(press_col.at[0], press_from_north, edge_sems, 5, 0, -1),
-    ]
+        send(press_row, press_from_east, edge_sems, 4, -1, 0),
+        send(press_col, press_from_north, edge_sems, 5, 0, -1),
+    ]
+    by_level(levels, lambda k, x: forward(k, x, whole_rest), zero_rest)
+    x, tail, packed = by_level(levels, backward_rest, (zero_rest, zero_rest, zero_side))
+    tail_ref[:, LANES:] = tail
+    last_row_rest[...] -= tail[rows - 1 :, :]
+    last_col[...] = packed - tail[:, rest - 1 :]
 
     totals[...] = jnp.zeros(totals.shape, F32)
 
@@ -477,9 +508,10 @@
 
     for copy in press:
         copy.wait()
-    speed_e = row_east[1] + (press_row[1] - press_from_east[...])
+    last_row = jnp.concatenate([last_row_low[...], last_row_rest[...]], axis=1)
+    speed_e = row_east[1] + (last_row - press_from_east[...])
     speed_e = jnp.where(level_row < last_e, speed_e, 0.0)
-    speed_n = pltpu.roll(col_north[...], HALF, 1) + (press_col[1] - press_from_north[...])
+    speed_n = pltpu.roll(col_north[...], HALF, 1) + (last_col[...] - press_from_north[...])
     speed_n = jnp.where(level_lane < last_n, speed_n, 0.0)
     fix_row[...] = speed_e
     fix_col[...] = speed_n
@@ -551,7 +583,6 @@
     row_set = pltpu.VMEM((levels, cols), F32)
     row_sets = pltpu.VMEM((2, levels, cols), F32)
     col_set = pltpu.VMEM((rows, LANES), F32)
-    col_sets = pltpu.VMEM((2, rows, LANES), F32)
     inputs = [
         pltpu.with_memory_space_constraint(array, pltpu.HBM)
         for array in (temp, speeds, mix, sea, tally, rain)
@@ -567,7 +598,8 @@
         + [two_planes, two_planes, plane]
         + [row_sets, row_set, row_sets, row_set]
         + [col_set] * 4
-        + [row_sets, row_set, col_sets, col_set]
+        + [row_set, row_set, col_set, col_set]
+        + [pltpu.VMEM((levels, LANES), F32), pltpu.VMEM((levels, cols - LANES), F32), col_set]
         + [row_set, col_set]
         + [
             pltpu.SemaphoreType.DMA((6,)),

time: 29.3 us -> 28.5 us (0.973)
  Pallas kernels: 28.3 us -> 27.5 us
    pallas_call x1, Pallas kernels: 24.4 us -> 23.7 us  [local(): pl.pallas_call(columns_kernel, out_shape=[field, pltpu.VMEM((2, levels, r...]
where the time goes in v7:
time: 28.5 us; the launch traced here: 28.2 us
  Pallas kernels  27.5 us (96%)
  between operations  0.64 us (2%)
    pallas_call x1, Pallas kernels, local(): pl.pallas_call(columns_kernel, out_shape=[field, pltpu.VMEM((2, levels, r...  23.7 us
    pallas_call x1, Pallas kernels, local(): pl.pallas_call(surface_kernel, out_shape=[jax.ShapeDtypeStruct(temp.shape...  3.89 us

profile of v7, /device:TPU:0, one launch (start us, length us, event | category | flops | bytes accessed | tf_op | source)
XLA Modules:
  0.0 28.2 jit_solution(13841648637909729672)
XLA Ops:
  0.6 23.7 %columns.1 = (f32[40,64,256]{2,1,0:T(8,128)S(1)}, f32[2,40,64,256]{3,2,1,0:T(8,128)S(1)}, f32[80,384]{1,0:T(8,128)S(1)}, f32[80,384]{1,0:T(8,128)S(1)}, f32[80,384]{1,0:T(8,128)S(1)}) custom-call(f32[40,64,256]{2,1,0:T(8,128)} %temp_hbm.1, f32[2,40,64,256]{3,2,1,0:T(8,128)} %speed_hbm.1, f32[40,64,256]{2,1,0:T(8,128)} %mix_hbm.1, s32[64,256]{1,0:T(8,128)} %sea_hbm.1, ...), custom_call_target="tpu_custom_call" | custom-call | tf_op jit(solution)/shard_map/columns/pallas_call | solution.py:590
  24.3 3.9 %surface.1 = (f32[40,64,256]{2,1,0:T(8,128)}, f32[2,40,64,256]{3,2,1,0:T(8,128)}, f32[64,256]{1,0:T(8,128)}) custom-call(f32[40,64,256]{2,1,0:T(8,128)S(1)} %get-tuple-element.8.temp_in, f32[2,40,64,256]{3,2,1,0:T(8,128)S(1)} %get-tuple-element.9.speed_in, f32[80,384]{1,0:T(8,128)S(1)} %get-tuple-element.10.root_in, ...), custom_call_target="tpu_custom_call" | custom-call | tf_op jit(solution)/shard_map/surface/pallas_call | solution.py:619

commit v8 on v7

--- a/solution.py
+++ b/solution.py
@@ -152,8 +152,9 @@
     temp_out,
     speed_out,
     root_out,
-    ratio_out,
-    scaled_out,
+    inverse_out,
+    source_out,
+    totals_out,
     temp,
     east,
     north,
@@ -211,15 +212,19 @@
                 (sea_hbm, sea),
                 (tally_hbm, tally),
                 (rain_hbm, surf.at[1]),
-                (temp_hbm, temp),
                 (speed_hbm.at[1, :, :, last_lanes], north.at[:, :, last_lanes]),
                 (speed_hbm.at[0, :, last_rows, :], east.at[:, last_rows, :]),
             )
         )
     ]
-    for copy in first_loads:
+    chunks = levels // GROUP
+
+    def load_temp(at):
+        span = pl.ds(at * GROUP, GROUP)
+        return pltpu.make_async_copy(temp_hbm.at[span], temp.at[span], chunk_sems.at[3, at])
+
+    for copy in first_loads[:3] + [load_temp(at) for at in range(chunks)] + first_loads[3:]:
         copy.start()
-    chunks = levels // GROUP
 
     def load_mix(at):
         span = pl.ds(at * GROUP, GROUP)
@@ -274,8 +279,13 @@
         row_east[1, pl.ds(k, 1), :] = east[k, rows - 1 : rows, :]
         return fill(k + HALF, to_north, lane, north[k, :, high], k + 1 + HALF)
 
-    first_loads[3].wait()
-    to_north, to_south = by_level(levels, pack_temp, (zero_side, zero_side))
+    def pack_chunk(at, carry):
+        load_temp(at).wait()
+        for inner in range(GROUP):
+            carry = pack_temp(at * GROUP + inner, carry)
+        return carry
+
+    to_north, to_south = lax.fori_loop(0, chunks, pack_chunk, (zero_side, zero_side))
     col_south[...] = to_south
     meet_neighbours()
     surf_copies = start_halo(surf, bands, sides, corners, halo_sems)
@@ -283,8 +293,8 @@
         send(row_west, from_east, edge_sems, 0, -1, 0),
         send(col_south, from_north, edge_sems, 1, 0, -1),
     ]
+    first_loads[3].wait()
     first_loads[4].wait()
-    first_loads[5].wait()
     col_north[...] = by_level(levels, pack_speed, to_north)
     edges += [
         send(row_east, from_west, edge_sems, 2, 1, 0),
@@ -530,25 +540,32 @@
 
     by_level(levels, add_last, 0)
 
-    source = source_scale * joined(1, surf, bands, sides, corners)
     root = jnp.sqrt(wide / levels)
     inverse = 1.0 / (damping + root * around_total(root))
     root_out[...] = root
-    ratio_out[...] = root * inverse
+    inverse_out[...] = inverse
+    source_out[...] = source_scale * joined(1, surf, bands, sides, corners)
 
     for copy in total_copies:
         copy.wait()
-    total_e = joined(0, totals, total_bands, total_sides, total_corners)
-    total_n = joined(1, totals, total_bands, total_sides, total_corners)
-    divergence = total_e - before(total_e, 0) + total_n - before(total_n, 1)
-    forcing = source - (divergence_scale / levels) * divergence
-    scaled_out[...] = jnp.where(root > 0.0, forcing * inverse, 0.0)
+    for which in range(2):
+        totals_out[which] = joined(which, totals, total_bands, total_sides, total_corners)
 
 
 def surface_kernel(
-    temp_in, speed_in, root_in, ratio_in, scaled_in, temp_out, speed_out, out, sems
+    temp_in,
+    speed_in,
+    root_in,
+    inverse_in,
+    source_in,
+    totals_in,
+    temp_out,
+    speed_out,
+    out,
+    sems,
 ):
     rows, cols = out.shape
+    levels = temp_in.shape[0]
     copies = [
         pltpu.make_async_copy(temp_in, temp_out, sems.at[0]),
         pltpu.make_async_copy(speed_in.at[0], speed_out.at[0], sems.at[1]),
@@ -557,8 +574,12 @@
     for copy in copies:
         copy.start()
     root = root_in[...]
-    ratio = ratio_in[...]
-    scaled = scaled_in[...]
+    inverse = inverse_in[...]
+    ratio = root * inverse
+    total_e, total_n = totals_in[0], totals_in[1]
+    divergence = total_e - before(total_e, 0) + total_n - before(total_n, 1)
+    forcing = source_in[...] - (divergence_scale / levels) * divergence
+    scaled = jnp.where(root > 0.0, forcing * inverse, 0.0)
     update = scaled * (1.0 / cheb_gamma)
     iterate = update
     omega = 2.0 / cheb_gamma
@@ -575,6 +596,7 @@
 def local(temp, speeds, mix, sea, tally, rain):
     levels, rows, cols = temp.shape
     wide = pltpu.VMEM((rows + 2 * BAND, cols + LANES), F32)
+    wide_pair = pltpu.VMEM((2, rows + 2 * BAND, cols + LANES), F32)
     vmem = pl.BlockSpec(memory_space=pltpu.VMEM)
     field = pltpu.VMEM((levels, rows, cols), F32)
     plane = pltpu.VMEM((rows, cols), F32)
@@ -587,11 +609,11 @@
         pltpu.with_memory_space_constraint(array, pltpu.HBM)
         for array in (temp, speeds, mix, sea, tally, rain)
     ]
-    temp_next, speed_next, root, ratio, scaled = pl.pallas_call(
+    results = pl.pallas_call(
         columns_kernel,
-        out_shape=[field, pltpu.VMEM((2, levels, rows, cols), F32), wide, wide, wide],
+        out_shape=[field, pltpu.VMEM((2, levels, rows, cols), F32), wide, wide, wide, wide_pair],
         in_specs=[pl.BlockSpec(memory_space=pltpu.HBM)] * 6,
-        out_specs=[vmem] * 5,
+        out_specs=[vmem] * 6,
         scratch_shapes=[field] * 7
         + [plane_int] * 2
         + [plane] * 3
@@ -602,8 +624,8 @@
         + [pltpu.VMEM((levels, LANES), F32), pltpu.VMEM((levels, cols - LANES), F32), col_set]
         + [row_set, col_set]
         + [
-            pltpu.SemaphoreType.DMA((6,)),
-            pltpu.SemaphoreType.DMA((3, levels // GROUP)),
+            pltpu.SemaphoreType.DMA((5,)),
+            pltpu.SemaphoreType.DMA((4, levels // GROUP)),
             pltpu.SemaphoreType.DMA((2, 6)),
         ]
         + halo_shapes(rows, cols) * 2,
@@ -614,7 +636,7 @@
     )(*inputs)
     held = [
         pltpu.with_memory_space_constraint(array, pltpu.VMEM)
-        for array in (temp_next, speed_next, root, ratio, scaled)
+        for array in results
     ]
     return pl.pallas_call(
         surface_kernel,
@@ -623,7 +645,7 @@
             jax.ShapeDtypeStruct(speeds.shape, F32),
             jax.ShapeDtypeStruct((rows, cols), F32),
         ],
-        in_specs=[vmem] * 5,
+        in_specs=[vmem] * 6,
         out_specs=[pl.BlockSpec(memory_space=pltpu.HBM)] * 2 + [vmem],
         scratch_shapes=[pltpu.SemaphoreType.DMA((3,))],
         compiler_params=pltpu.CompilerParams(vmem_limit_bytes=32 * 2**20),

time: 28.5 us -> 28.1 us (0.986)
  Pallas kernels: 27.5 us -> 27.1 us
    pallas_call x1, Pallas kernels: 23.7 us -> 23.2 us  [local(): pl.pallas_call(columns_kernel, out_shape=[field, pltpu.VMEM((2, levels, r...]
where the time goes in v8:
time: 28.1 us; the launch traced here: 27.7 us
  Pallas kernels  27.1 us (96%)
  between operations  0.64 us (2%)
    pallas_call x1, Pallas kernels, local(): pl.pallas_call(columns_kernel, out_shape=[field, pltpu.VMEM((2, levels, r...  23.2 us
    pallas_call x1, Pallas kernels, local(): pl.pallas_call(surface_kernel, out_shape=[jax.ShapeDtypeStruct(temp.shape...  3.89 us

profile of v8, /device:TPU:0, one launch (start us, length us, event | category | flops | bytes accessed | tf_op | source)
XLA Modules:
  0.0 27.7 jit_solution(11415928872170763846)
XLA Ops:
  0.6 23.2 %columns.1 = (f32[40,64,256]{2,1,0:T(8,128)S(1)}, f32[2,40,64,256]{3,2,1,0:T(8,128)S(1)}, f32[80,384]{1,0:T(8,128)S(1)}, f32[80,384]{1,0:T(8,128)S(1)}, f32[80,3...) custom-call(f32[40,64,256]{2,1,0:T(8,128)} %temp_hbm.1, f32[2,40,64,256]{3,2,1,0:T(8,128)} %speed_hbm.1, f32[40,64,256]{2,1,0:T(8,128)} %mix_hbm.1, ...), custom_call_target="tpu_custom_call" | custom-call | tf_op jit(solution)/shard_map/columns/pallas_call | solution.py:612
  23.9 3.9 %surface.1 = (f32[40,64,256]{2,1,0:T(8,128)}, f32[2,40,64,256]{3,2,1,0:T(8,128)}, f32[64,256]{1,0:T(8,128)}) custom-call(f32[40,64,256]{2,1,0:T(8,128)S(1)} %get-tuple-element.9.temp_in, f32[2,40,64,256]{3,2,1,0:T(8,128)S(1)} %get-tuple-element.10.speed_in, f32[80,384]{1,0:T(8,128)S(1)} %get-tuple-element.11.root_in, ...), custom_call_target="tpu_custom_call" | custom-call | tf_op jit(solution)/shard_map/surface/pallas_call | solution.py:641
